TPU v7x, 256 devices: a whole 4x4x8 slice. The times are simulated.
256 devices in a mesh: dp: 8 (over y, z_lo), expert: 32 (over z_hi, x, core).
Axes of the slice: x: 4, y: 4, z: 8 (z_hi: 4, z_lo: 2; z = z_hi * 2 + z_lo), core: 2. Of those that a mesh axis runs over, the one named last changes fastest.
Arguments:
- tokens: bfloat16 [65536, 1024], P(('dp', 'expert')), may hold values from -6 to 6
- cotangent: bfloat16 [65536, 1024], P(('dp', 'expert')), may hold values from -1.1953125 to 1.1953125
- prob: bfloat16 [65536], P(('dp', 'expert')), may hold values from 0.19921875 to 1
- assign: int32 [65536, 1], P(('dp', 'expert')), may hold values from 0 to 31; in each aligned block of 256 rows (0 to 255, 256 to 511, ...) at most 24 rows name the same one
- w_gate: bfloat16 [32, 1024, 1024], P('expert'), may hold values from -0.1875 to 0.1875
- w_up: bfloat16 [32, 1024, 1024], P('expert'), may hold values from -0.1875 to 0.1875
- w_down: bfloat16 [32, 1024, 1024], P('expert'), may hold values from -0.1875 to 0.1875
Outputs:
- grad_tokens: bfloat16 [65536, 1024], P(('dp', 'expert'))
- grad_prob: bfloat16 [65536], P(('dp', 'expert'))
- grad_gate: float32 [32, 1024, 1024], P('expert', 'dp')
- grad_up: float32 [32, 1024, 1024], P('expert', 'dp')
- grad_down: float32 [32, 1024, 1024], P('expert', 'dp')
Inputs may be any that keep to these rules, and one draw needn't show every extreme that they name: `assign`: among the 256 tokens of one device (aligned blocks of rows), at most 24 are assigned to one expert, and in every draw some expert receives exactly 24 tokens of some device.
All inputs are finite; a program needn't handle non-finite values.
Results may differ from a plain program's by a relative error of at most 0.015.
Values may be sent and summed in bfloat16 or wider, within the bound.
No kernel may reach another device: no remote copies, remote signals or barrier semaphores. Data moves between devices by JAX's collectives and lax.ppermute only.
A program may use at most 128 MiB of HBM per device.

v0:
```python
import jax
import jax.numpy as jnp
from jax import lax
from jax.sharding import PartitionSpec as P


def placement_of(assign_dev, experts, capacity):
    chosen = (assign_dev[:, None] == jnp.arange(experts, dtype=jnp.int32)[None, :]).astype(
        jnp.int32
    )
    before = jnp.cumsum(chosen, axis=0) - chosen
    position = jnp.sum(before * chosen, axis=1)
    slot = assign_dev * capacity + position
    return jnp.arange(experts * capacity, dtype=jnp.int32)[:, None] == slot[None, :]


def recompute(rows_in, gate_weight, up_weight, down_weight):
    gate = jnp.dot(rows_in, gate_weight, preferred_element_type=jnp.float32)
    up = jnp.dot(rows_in, up_weight, preferred_element_type=jnp.float32)
    sigmoid_gate = jax.nn.sigmoid(gate)
    activation = gate * sigmoid_gate
    hidden = (activation * up).astype(jnp.bfloat16)
    expert_out = jnp.dot(hidden, down_weight, preferred_element_type=jnp.float32)
    return (gate, up, sigmoid_gate, activation, hidden, expert_out)


def local(tokens, cotangent, prob, assign, w_gate, w_up, w_down):
    experts = lax.axis_size("expert")
    tok_rows = tokens.shape[0]
    width = tokens.shape[1]
    capacity = 3 * tok_rows // experts
    slots_all = experts * capacity
    gate_weight = w_gate[0]
    up_weight = w_up[0]
    down_weight = w_down[0]
    place = placement_of(assign[:, 0], experts, capacity)
    weights = place.astype(jnp.bfloat16)
    send_rows = (
        jnp.dot(weights, tokens, preferred_element_type=jnp.float32)
        .astype(jnp.bfloat16)
        .reshape(experts, capacity, width)
    )
    send_cot = (
        jnp.dot(weights, cotangent, preferred_element_type=jnp.float32)
        .astype(jnp.bfloat16)
        .reshape(experts, capacity, width)
    )
    send_prob = (
        jnp.sum(jnp.where(place, prob[None, :].astype(jnp.float32), 0.0), axis=1)
        .astype(jnp.bfloat16)
        .reshape(experts, capacity)
    )
    recv_rows, recv_cot, recv_prob = (
        lax.all_to_all(send_rows, "expert", split_axis=0, concat_axis=0, tiled=True),
        lax.all_to_all(send_cot, "expert", split_axis=0, concat_axis=0, tiled=True),
        lax.all_to_all(send_prob, "expert", split_axis=0, concat_axis=0, tiled=True),
    )
    rows_in = recv_rows.reshape(slots_all, width)
    gate, up, sigmoid_gate, activation, hidden, expert_out = recompute(
        rows_in, gate_weight, up_weight, down_weight
    )
    cot_in = recv_cot.reshape(slots_all, width)
    prob_in = recv_prob.reshape(slots_all)
    grad_pr = jnp.sum(cot_in.astype(jnp.float32) * expert_out, axis=1).astype(jnp.bfloat16)
    scaled = (prob_in.astype(jnp.float32)[:, None] * cot_in.astype(jnp.float32)).astype(
        jnp.bfloat16
    )
    grad_hidden = lax.dot_general(
        scaled, down_weight, (((1,), (1,)), ((), ())), preferred_element_type=jnp.float32
    )
    grad_gate_pre = (grad_hidden * up * sigmoid_gate * (1.0 + gate * (1.0 - sigmoid_gate))).astype(
        jnp.bfloat16
    )
    grad_up_pre = (grad_hidden * activation).astype(jnp.bfloat16)
    grad_rows = lax.dot_general(
        grad_gate_pre, gate_weight, (((1,), (1,)), ((), ())), preferred_element_type=jnp.float32
    )
    grad_rows = grad_rows + lax.dot_general(
        grad_up_pre, up_weight, (((1,), (1,)), ((), ())), preferred_element_type=jnp.float32
    )
    grad_rows = grad_rows.astype(jnp.bfloat16)
    back_rows, back_prob = (
        lax.all_to_all(
            grad_rows.reshape(experts, capacity, width),
            "expert",
            split_axis=0,
            concat_axis=0,
            tiled=True,
        ),
        lax.all_to_all(
            grad_pr.reshape(experts, capacity), "expert", split_axis=0, concat_axis=0, tiled=True
        ),
    )
    grad_tokens = lax.dot_general(
        weights,
        back_rows.reshape(slots_all, width),
        (((0,), (0,)), ((), ())),
        preferred_element_type=jnp.float32,
    ).astype(jnp.bfloat16)
    grad_prob = jnp.sum(
        jnp.where(place, back_prob.reshape(slots_all)[:, None].astype(jnp.float32), 0.0), axis=0
    ).astype(jnp.bfloat16)
    part_gate = lax.dot_general(
        rows_in, grad_gate_pre, (((0,), (0,)), ((), ())), preferred_element_type=jnp.float32
    )
    part_up = lax.dot_general(
        rows_in, grad_up_pre, (((0,), (0,)), ((), ())), preferred_element_type=jnp.float32
    )
    part_down = lax.dot_general(
        hidden, scaled, (((0,), (0,)), ((), ())), preferred_element_type=jnp.float32
    )
    grad_gate, grad_up, grad_down = (
        lax.psum_scatter(
            part_gate[None].astype(jnp.bfloat16), "dp", scatter_dimension=1, tiled=True
        ).astype(jnp.float32),
        lax.psum_scatter(
            part_up[None].astype(jnp.bfloat16), "dp", scatter_dimension=1, tiled=True
        ).astype(jnp.float32),
        lax.psum_scatter(
            part_down[None].astype(jnp.bfloat16), "dp", scatter_dimension=1, tiled=True
        ).astype(jnp.float32),
    )
    return (grad_tokens, grad_prob, grad_gate, grad_up, grad_down)


def solution(mesh):
    placed = (
        P(("dp", "expert"), None),
        P(("dp", "expert"), None),
        P(("dp", "expert")),
        P(("dp", "expert"), None),
        P("expert", None, None),
        P("expert", None, None),
        P("expert", None, None),
    )
    return jax.shard_map(
        local,
        mesh=mesh,
        in_specs=placed,
        out_specs=(
            P(("dp", "expert"), None),
            P(("dp", "expert")),
            P("expert", "dp", None),
            P("expert", "dp", None),
            P("expert", "dp", None),
        ),
        check_vma=False,
    )
```

profile of v0, /device:TPU:1, one launch (start us, length us, event | category | flops | bytes accessed | tf_op | source)
XLA Modules:
  0.0 354.9 jit_solution(7641260826526963940)
XLA Ops:
  7.2 0.8 fusion.26
  8.0 0.6 reduce-window.6
  8.6 0.2 slice_reduce_fusion
  8.8 0.8 fusion.25
  9.6 0.7 multiply_add_fusion
  10.3 2.8 convolution_convert_fusion
  13.1 12.8 %all-to-all-start.2 = ((bf16[32,24,1024]{2,1,0:T(8,128)(2,1)}), bf16[32,24,1024]{2,1,0:T(8,128)(2,1)}, u32[]{:S(2)}, u32[]{:S(2)}) async-start(bf16[32,24,1024]{2,1,0:T(8,128)(2,1)} %bitcast.80), calls=%async_computation.2 | async-start | bytes 3145728 | tf_op jit(solution)/shard_map/all_to_all | solution.py:54
  25.8 1.7 convolution_convert_fusion.1
  27.6 37.1 %all-to-all-done.2 = bf16[32,24,1024]{2,1,0:T(8,128)(2,1)} async-done(((bf16[32,24,1024]{2,1,0:T(8,128)(2,1)}), bf16[32,24,1024]{2,1,0:T(8,128)(2,1)}, u32[]{:S(2)}, u32[]{:S(2)}) %all-to-all-start.2) | async-done | bytes 1572896 | tf_op jit(solution)/shard_map/all_to_all | solution.py:54
  64.6 6.7 %all-to-all-start.1 = ((bf16[32,24,1024]{2,1,0:T(8,128)(2,1)}), bf16[32,24,1024]{2,1,0:T(8,128)(2,1)}, u32[]{:S(2)}, u32[]{:S(2)}) async-start(bf16[32,24,1024]{2,1,0:T(8,128)(2,1)} %bitcast.79), calls=%async_computation.1 | async-start | bytes 3145728 | tf_op jit(solution)/shard_map/all_to_all | solution.py:55
  71.3 3.9 %fusion.6 = f32[768,1024]{1,0:T(8,128)S(1)} fusion(bf16[768,1024]{1,0:T(8,128)(2,1)} %bitcast.8, bf16[1,1024,1024]{2,1,0:T(8,128)(2,1)} %param.11), kind=kOutput, calls=%fused_computation.14 | convolution fusion | flops 1610612736 | bytes 6815744 | tf_op jit(solution)/shard_map/dot_general | solution.py:18
  75.2 1.7 copy-done.4
  76.8 5.6 %multiply_convert_fusion = (bf16[768,1024]{1,0:T(8,128)(2,1)}, f32[768,1024]{1,0:T(8,128)}) fusion(f32[768,1024]{1,0:T(8,128)S(1)} %fusion.6, bf16[768,1024]{1,0:T(8,128)(2,1)} %bitcast.8, bf16[1,1024,1024]{2,1,0:T(8,128)(2,1)S(1)} %copy-done), kind=kOutput, calls=%fused_computation.6 | convolution fusion | flops 1615331328 | bytes 11534336 | tf_op jit(solution)/shard_map/dot_general | solution.py:19
  82.4 27.9 %all-to-all-done.1 = bf16[32,24,1024]{2,1,0:T(8,128)(2,1)} async-done(((bf16[32,24,1024]{2,1,0:T(8,128)(2,1)}), bf16[32,24,1024]{2,1,0:T(8,128)(2,1)}, u32[]{:S(2)}, u32[]{:S(2)}) %all-to-all-start.1) | async-done | bytes 1572896 | tf_op jit(solution)/shard_map/all_to_all | solution.py:55
  110.4 4.4 %fusion.1 = bf16[768]{0:T(1024)(128)(2,1)S(1)} fusion(bf16[32,24,1024]{2,1,0:T(8,128)(2,1)} %all-to-all-done.1, bf16[768,1024]{1,0:T(8,128)(2,1)} %get-tuple-element.9, bf16[1,1024,1024]{2,1,0:T(8,128)(2,1)} %param.13), kind=kOutput, calls=%fused_computation.4 | convolution fusion | flops 1612971264 | bytes 5244416 | tf_op jit(solution)/shard_map/dot_general | solution.py:23
  114.7 0.7 convert_element_type.177
  115.5 6.4 %all-to-all-start.4 = ((bf16[32,1,24]{2,1,0:T(2,128)(2,1)}), bf16[32,1,24]{2,1,0:T(2,128)(2,1)S(1)}, u32[]{:S(2)}, u32[]{:S(2)}) async-start(bf16[32,1,24]{2,1,0:T(2,128)(2,1)} %convert_element_type.177), calls=%async_computation.4 | async-start | bytes 32768 | tf_op jit(solution)/shard_map/all_to_all | solution.py:90
  121.9 0.0 reduce-scatter.8.cloned.1.call-start
  122.0 9.2 %all-to-all-done.4 = bf16[32,1,24]{2,1,0:T(2,128)(2,1)S(1)} async-done(((bf16[32,1,24]{2,1,0:T(2,128)(2,1)}), bf16[32,1,24]{2,1,0:T(2,128)(2,1)S(1)}, u32[]{:S(2)}, u32[]{:S(2)}) %all-to-all-start.4) | async-done | bytes 1568 | tf_op jit(solution)/shard_map/all_to_all | solution.py:90
  131.2 0.1 convert_reduce_fusion
  131.3 0.1 reshape.123
  131.3 0.8 select_reduce_fusion
  132.1 0.1 convert_element_type.176
  132.2 12.7 %all_to_all.27 = bf16[32,1,24]{2,1,0:T(2,128)(2,1)S(1)} all-to-all(bf16[32,1,24]{2,1,0:T(2,128)(2,1)S(1)} %convert_element_type.176), channel_id=1, replica_groups=mesh['dp'=8,'expert'=32] {'expert'}, dimensions={0} | all-to-all | bytes 3072 | tf_op jit(solution)/shard_map/all_to_all | solution.py:56
  144.9 0.1 convert_reduce_fusion.1
  145.0 0.1 reshape.124
  145.1 1.8 fusion.2
  146.9 0.0 copy-done.7
  146.9 3.2 convert_bitcast_fusion
  150.1 0.0 reduce-scatter.8.cloned.1.call-update
  150.2 0.2 reduce-scatter.6.cloned.1.call-start
  150.4 1.9 fusion
  152.3 0.1 copy-done.2
  152.5 6.7 %multiply_convert_fusion.1 = (bf16[768,1024]{1,0:T(8,128)(2,1)S(1)}, bf16[768,1024]{1,0:T(8,128)(2,1)}) fusion(f32[768,1024]{1,0:T(8,128)} %copy-done.4, f32[768,1024]{1,0:T(8,128)} %get-tuple-element.10, bf16[768,1024]{1,0:T(8,128)(2,1)S(1)} %bitcast.81, bf16[1,1024,1024]{2,1,0:T(8,128)(2,1)S(1)} %copy-done.2), kind=kOutput, calls=%fused_computation.8 | convolution fusion | flops 1620836352 | bytes 13107200 | tf_op jit(solution)/shard_map/dot_general | solution.py:68
  159.2 1.2 copy-done.5
  160.3 4.6 %convert_bitcast_fusion.1 = bf16[1,1024,1024]{2,1,0:T(8,128)(2,1)} fusion(bf16[768,1024]{1,0:T(8,128)(2,1)} %bitcast.8, bf16[768,1024]{1,0:T(8,128)(2,1)S(1)} %get-tuple-element.7), kind=kOutput, calls=%fused_computation.25 | convolution fusion | flops 1611661312 | bytes 5242880 | tf_op jit(solution)/shard_map/dot_general | solution.py:106
  164.9 0.0 reduce-scatter.6.cloned.1.call-update
  164.9 0.0 reduce-scatter.4.cloned.1.call-start
  165.0 5.1 %convert_bitcast_fusion.2 = bf16[1,1024,1024]{2,1,0:T(8,128)(2,1)} fusion(bf16[768,1024]{1,0:T(8,128)(2,1)} %bitcast.8, bf16[768,1024]{1,0:T(8,128)(2,1)} %get-tuple-element.8), kind=kOutput, calls=%fused_computation.26 | convolution fusion | flops 1611661312 | bytes 5242880 | tf_op jit(solution)/shard_map/dot_general | solution.py:103
  170.1 4.0 %fusion.4 = f32[768,1024]{1,0:T(8,128)S(1)} fusion(bf16[768,1024]{1,0:T(8,128)(2,1)} %get-tuple-element.8, bf16[1,1024,1024]{2,1,0:T(8,128)(2,1)} %param.11), kind=kOutput, calls=%fused_computation.12 | convolution fusion | flops 1610612736 | bytes 6815744 | tf_op jit(solution)/shard_map/dot_general | solution.py:75
  174.2 1.8 add_convert_fusion
  176.0 60.4 %all_to_all.28 = bf16[32,24,1024]{2,1,0:T(8,128)(2,1)S(1)} all-to-all(bf16[32,24,1024]{2,1,0:T(8,128)(2,1)S(1)} %bitcast.82), channel_id=1, replica_groups=mesh['dp'=8,'expert'=32] {'expert'}, dimensions={0} | all-to-all | bytes 3145728 | tf_op jit(solution)/shard_map/all_to_all | solution.py:83
  236.4 1.4 convolution_convert_fusion.2
  237.8 1.8 convert_element_type.171
  239.6 50.1 %reduce-scatter.6.cloned.1.call-done = bf16[1,128,1024]{2,1,0:T(8,128)(2,1)} async-done(((bf16[1,1024,1024]{2,1,0:T(8,128)(2,1)}), bf16[1,128,1024]{2,1,0:T(8,128)(2,1)}) %reduce-scatter.6.cloned.1.call-update) | async-done | bytes 262160 | tf_op jit(solution)/shard_map/reduce_scatter | solution.py:116
  289.7 1.8 convert_element_type.165
  291.5 55.1 %reduce-scatter.4.cloned.1.call-done = bf16[1,128,1024]{2,1,0:T(8,128)(2,1)} async-done(((bf16[1,1024,1024]{2,1,0:T(8,128)(2,1)}), bf16[1,128,1024]{2,1,0:T(8,128)(2,1)}) %reduce-scatter.4.cloned.1.call-update) | async-done | bytes 262160 | tf_op jit(solution)/shard_map/reduce_scatter | solution.py:113
  346.6 1.8 convert_element_type.162
  (18 shorter events, 0.1 us)
Async XLA Ops:
  7.2 69.7 %copy-start = (bf16[1,1024,1024]{2,1,0:T(8,128)(2,1)S(1)}, bf16[1,1024,1024]{2,1,0:T(8,128)(2,1)}, u32[]{:S(2)}) copy-start(bf16[1,1024,1024]{2,1,0:T(8,128)(2,1)} %param.12) | copy-start | bytes 6291460
  13.1 12.8 %copy-start.1 = (bf16[256,1024]{1,0:T(8,128)(2,1)S(1)}, bf16[256,1024]{1,0:T(8,128)(2,1)}, u32[]{:S(2)}) copy-start(bf16[256,1024]{1,0:T(8,128)(2,1)} %param.8) | copy-start | bytes 1572868
  13.1 51.6 %all-to-all-start.2 = ((bf16[32,24,1024]{2,1,0:T(8,128)(2,1)}), bf16[32,24,1024]{2,1,0:T(8,128)(2,1)}, u32[]{:S(2)}, u32[]{:S(2)}) async-start(bf16[32,24,1024]{2,1,0:T(8,128)(2,1)} %bitcast.80), calls=%async_computation.2 | async-start | bytes 3145728 | tf_op jit(solution)/shard_map/all_to_all | solution.py:54
  64.6 45.7 %all-to-all-start.1 = ((bf16[32,24,1024]{2,1,0:T(8,128)(2,1)}), bf16[32,24,1024]{2,1,0:T(8,128)(2,1)}, u32[]{:S(2)}, u32[]{:S(2)}) async-start(bf16[32,24,1024]{2,1,0:T(8,128)(2,1)} %bitcast.79), calls=%async_computation.1 | async-start | bytes 3145728 | tf_op jit(solution)/shard_map/all_to_all | solution.py:55
  75.2 1.7 copy-start.4
  110.3 11.6 %copy-start.3 = (bf16[256]{0:T(256)(128)(2,1)S(1)}, bf16[256]{0:T(256)(128)(2,1)}, u32[]{:S(2)}) copy-start(bf16[256]{0:T(256)(128)(2,1)} %param.9) | copy-start | bytes 1540
  115.5 15.7 %all-to-all-start.4 = ((bf16[32,1,24]{2,1,0:T(2,128)(2,1)}), bf16[32,1,24]{2,1,0:T(2,128)(2,1)S(1)}, u32[]{:S(2)}, u32[]{:S(2)}) async-start(bf16[32,1,24]{2,1,0:T(2,128)(2,1)} %convert_element_type.177), calls=%async_computation.4 | async-start | bytes 32768 | tf_op jit(solution)/shard_map/all_to_all | solution.py:90
  121.9 115.9 %reduce-scatter.8.cloned.1.call-start = ((), (), s32[]{:S(2)}) async-start(), calls=%async_computation.10 | async-start | bytes 2359296 | tf_op jit(solution)/shard_map/reduce_scatter | solution.py:119
  145.1 1.9 copy-start.7
  150.2 139.5 %reduce-scatter.6.cloned.1.call-start = ((), (), s32[]{:S(2)}) async-start(), calls=%async_computation.9 | async-start | bytes 2359296 | tf_op jit(solution)/shard_map/reduce_scatter | solution.py:116
  150.4 2.1 copy-start.2
  159.2 1.2 copy-start.5
  164.9 181.6 %reduce-scatter.4.cloned.1.call-start = ((), (), s32[]{:S(2)}) async-start(), calls=%async_computation.8 | async-start | bytes 2359296 | tf_op jit(solution)/shard_map/reduce_scatter | solution.py:113
  170.1 4.0 %copy-start.6 = (bf16[768,1024]{1,0:T(8,128)(2,1)S(1)}, bf16[768,1024]{1,0:T(8,128)(2,1)}, u32[]{:S(2)}) copy-start(bf16[768,1024]{1,0:T(8,128)(2,1)} %copy-done.5) | copy-start | bytes 4718596
Sparse Core Ops, SparseCore 0:
  150.3 80.4 reduce-scatter.7
  233.3 56.3 reduce-scatter.5
  292.2 54.2 reduce-scatter.3
where the time goes:
time: 356 us; the launch traced here: 355 us
  waiting for transfers between devices  179 us (50%)
  blocking collectives  73.1 us (21%)
  matrix products  45.2 us (13%)
  starting transfers between devices  26.2 us (7%)
  between operations  13.9 us (4%)
  other arithmetic  12.9 us (4%)
  local copies, waits for them, and re-layouts  4.18 us (1%)
    all_to_all x1, blocking collectives, local(): lax.all_to_all(grad_rows.reshape(experts, capacity, width), 'expert', spl...  60.4 us
    reduce_scatter x1, waiting for transfers between devices, local(): lax.psum_scatter(part_gate[None].astype(jnp.bfloat16), 'dp', scatter_dime...  55.1 us
    reduce_scatter x1, waiting for transfers between devices, local(): lax.psum_scatter(part_up[None].astype(jnp.bfloat16), 'dp', scatter_dimens...  50.1 us
    all_to_all x1, waiting for transfers between devices, local(): lax.all_to_all(send_rows, 'expert', split_axis=0, concat_axis=0, tiled=True)  37.1 us
    all_to_all x1, waiting for transfers between devices, local(): lax.all_to_all(send_cot, 'expert', split_axis=0, concat_axis=0, tiled=True)  27.9 us
    all_to_all x1, starting transfers between devices, local(): lax.all_to_all(send_rows, 'expert', split_axis=0, concat_axis=0, tiled=True)  12.8 us
    all_to_all x1, blocking collectives, local(): lax.all_to_all(send_prob, 'expert', split_axis=0, concat_axis=0, tiled=True)  12.7 us
    all_to_all x1, waiting for transfers between devices, local(): lax.all_to_all(grad_pr.reshape(experts, capacity), 'expert', split_axis=0...  9.24 us
  transfers between devices with their start and end apart: 6, of which 5 were waited for; matrix products, arithmetic and copies ran while one was open for 11% of the time, Pallas kernels for 0%

commit v1 on v0

--- a/solution.py
+++ b/solution.py
@@ -22,6 +22,58 @@
     hidden = (activation * up).astype(jnp.bfloat16)
     expert_out = jnp.dot(hidden, down_weight, preferred_element_type=jnp.float32)
     return (gate, up, sigmoid_gate, activation, hidden, expert_out)
+
+
+AXES = ("dp", "expert")
+
+
+def shift_y(value, step):
+    pairs = []
+    for dp in range(8):
+        y, low = divmod(dp, 2)
+        pairs.append((dp, ((y + step) % 4) * 2 + low))
+    return lax.ppermute(value, "dp", pairs)
+
+
+def swap_low(value):
+    return lax.ppermute(value, "dp", [(dp, dp ^ 1) for dp in range(8)])
+
+
+def summed_parts(pairs):
+    index = lax.axis_index("dp")
+    y, low = index // 2, index % 2
+    half = 512
+
+    def chunk(pair, offset):
+        left, right = pair
+        start = ((y + offset) % 4) * 256
+        piece = lax.dynamic_slice_in_dim(left, start, 256, axis=1)
+        return lax.dot_general(
+            piece, right, (((0,), (0,)), ((), ())), preferred_element_type=jnp.float32
+        )
+
+    far = [chunk(pair, 2).astype(jnp.bfloat16) for pair in pairs]
+    first = [(shift_y(f[:, :half], 1), shift_y(f[:, half:], -1)) for f in far]
+    second = []
+    for pair, (from_left, from_right) in zip(pairs, first):
+        up_part = chunk(pair, 1)
+        down_part = chunk(pair, 3)
+        up_part = jnp.concatenate(
+            [up_part[:, :half] + from_left.astype(jnp.float32), up_part[:, half:]], axis=1
+        ).astype(jnp.bfloat16)
+        down_part = jnp.concatenate(
+            [down_part[:, :half], down_part[:, half:] + from_right.astype(jnp.float32)], axis=1
+        ).astype(jnp.bfloat16)
+        second.append((shift_y(up_part, 1), shift_y(down_part, -1)))
+    own = [chunk(pair, 0) for pair in pairs]
+    results = []
+    for mine, (from_left, from_right) in zip(own, second):
+        total = mine + from_left.astype(jnp.float32) + from_right.astype(jnp.float32)
+        away = lax.dynamic_slice_in_dim(total, (1 - low) * 128, 128, axis=0)
+        keep = lax.dynamic_slice_in_dim(total, low * 128, 128, axis=0)
+        other = swap_low(away.astype(jnp.bfloat16))
+        results.append((keep + other.astype(jnp.float32))[None])
+    return results
 
 
 def local(tokens, cotangent, prob, assign, w_gate, w_up, w_down):
@@ -100,25 +152,8 @@
     grad_prob = jnp.sum(
         jnp.where(place, back_prob.reshape(slots_all)[:, None].astype(jnp.float32), 0.0), axis=0
     ).astype(jnp.bfloat16)
-    part_gate = lax.dot_general(
-        rows_in, grad_gate_pre, (((0,), (0,)), ((), ())), preferred_element_type=jnp.float32
-    )
-    part_up = lax.dot_general(
-        rows_in, grad_up_pre, (((0,), (0,)), ((), ())), preferred_element_type=jnp.float32
-    )
-    part_down = lax.dot_general(
-        hidden, scaled, (((0,), (0,)), ((), ())), preferred_element_type=jnp.float32
-    )
-    grad_gate, grad_up, grad_down = (
-        lax.psum_scatter(
-            part_gate[None].astype(jnp.bfloat16), "dp", scatter_dimension=1, tiled=True
-        ).astype(jnp.float32),
-        lax.psum_scatter(
-            part_up[None].astype(jnp.bfloat16), "dp", scatter_dimension=1, tiled=True
-        ).astype(jnp.float32),
-        lax.psum_scatter(
-            part_down[None].astype(jnp.bfloat16), "dp", scatter_dimension=1, tiled=True
-        ).astype(jnp.float32),
+    grad_down, grad_gate, grad_up = summed_parts(
+        ((hidden, scaled), (rows_in, grad_gate_pre), (rows_in, grad_up_pre))
     )
     return (grad_tokens, grad_prob, grad_gate, grad_up, grad_down)
 

time: 356 us -> 244 us (0.69)
  blocking collectives: 73.1 us -> 0 us
  waiting for transfers between devices: 179 us -> 113 us
  starting transfers between devices: 26.2 us -> 52.2 us
  between operations: 13.9 us -> 1.49 us
  local copies, waits for them, and re-layouts: 4.18 us -> 10.3 us
  other arithmetic: 12.9 us -> 17.3 us
    reduce_scatter x3 -> x0, waiting for transfers between devices: 105 us -> none  [the longest x1 55.1 us: local(): lax.psum_scatter(part_gate[None].astype(jnp.bfloat16), 'dp', scatter_dime...]
    all_to_all x2 -> x0, blocking collectives: 73.1 us -> none  [the longest x1 60.4 us: local(): lax.all_to_all(grad_rows.reshape(experts, capacity, width), 'expert', spl...]
    ppermute x0 -> x15, waiting for transfers between devices: none -> 29.9 us  [the longest x12 25.7 us: shift_y(): return lax.ppermute(value, 'dp', pairs)]
    ppermute x0 -> x15, starting transfers between devices: none -> 16 us  [the longest x12 14.4 us: shift_y(): return lax.ppermute(value, 'dp', pairs)]
    all_to_all x0 -> x2, starting transfers between devices: none -> 9.9 us  [the longest x1 5.78 us: local(): lax.all_to_all(grad_rows.reshape(experts, capacity, width), 'expert', spl...]
    all_to_all x0 -> x2, waiting for transfers between devices: none -> 9.31 us  [the longest x1 9.3 us: local(): lax.all_to_all(send_prob, 'expert', split_axis=0, concat_axis=0, tiled=True)]
    slice x1 -> x10, local copies, waits for them, and re-layouts: 0.18 us -> 6.41 us  [the longest x3 2.49 us: summed_parts(): first = [(shift_y(f[:, :half], 1), shift_y(f[:, half:], -1)) for f in far]]
    convert_element_type x3 -> x0, other arithmetic: 5.38 us -> none  [local(): grad_gate, grad_up, grad_down = (lax.psum_scatter(part_gate[None].astype(...]
  transfers between devices with their start and end apart: 6 -> 20, of which waited for: 5 -> 12; matrix products, arithmetic and copies ran while one was open for 11% -> 13% of each run, Pallas kernels for 0% -> 0%
where the time goes in v1:
time: 244 us; the launch traced here: 241 us
  waiting for transfers between devices  113 us (46%)
  starting transfers between devices  52.2 us (21%)
  matrix products  46.8 us (19%)
  other arithmetic  17.3 us (7%)
  local copies, waits for them, and re-layouts  10.3 us (4%)
    all_to_all x1, waiting for transfers between devices, local(): lax.all_to_all(send_rows, 'expert', split_axis=0, concat_axis=0, tiled=True)  37 us
    all_to_all x1, waiting for transfers between devices, local(): lax.all_to_all(send_cot, 'expert', split_axis=0, concat_axis=0, tiled=True)  27.4 us
    ppermute x12, waiting for transfers between devices, shift_y(): return lax.ppermute(value, 'dp', pairs)  25.7 us
    dot_general x12, matrix products, chunk(): lax.dot_general(piece, right, (((0,), (0,)), ((), ())), preferred_element...  17.9 us
    ppermute x12, starting transfers between devices, shift_y(): return lax.ppermute(value, 'dp', pairs)  14.4 us
    all_to_all x1, starting transfers between devices, local(): lax.all_to_all(send_rows, 'expert', split_axis=0, concat_axis=0, tiled=True)  12.8 us
    all_to_all x1, waiting for transfers between devices, local(): lax.all_to_all(send_prob, 'expert', split_axis=0, concat_axis=0, tiled=True)  9.3 us
    all_to_all x1, waiting for transfers between devices, local(): lax.all_to_all(grad_pr.reshape(experts, capacity), 'expert', split_axis=0...  9.25 us
  transfers between devices with their start and end apart: 20, of which 12 were waited for; matrix products, arithmetic and copies ran while one was open for 13% of the time, Pallas kernels for 0%

profile of v1, /device:TPU:1, one launch (start us, length us, event | category | flops | bytes accessed | tf_op | source)
XLA Modules:
  0.0 241.0 jit_solution(4856486930758292665)
XLA Ops:
  3.7 2.9 %convolution_convert_fusion = bf16[768,1024]{1,0:T(8,128)(2,1)} fusion(bf16[256,1024]{1,0:T(8,128)(2,1)} %param.7, s32[256]{0:T(256)S(1)} %multiply_add_fusion), kind=kOutput, calls=%fused_computation.24 | convolution fusion | flops 403636224 | bytes 2098176 | tf_op jit(solution)/shard_map/dot_general | solution.py:91
  6.6 12.8 %all-to-all-start.2 = ((bf16[32,24,1024]{2,1,0:T(8,128)(2,1)}), bf16[32,24,1024]{2,1,0:T(8,128)(2,1)}, u32[]{:S(2)}, u32[]{:S(2)}) async-start(bf16[32,24,1024]{2,1,0:T(8,128)(2,1)} %bitcast.86), calls=%async_computation.2 | async-start | bytes 3145728 | tf_op jit(solution)/shard_map/all_to_all | solution.py:106
  19.4 1.7 convolution_convert_fusion.1
  21.1 37.0 %all-to-all-done.2 = bf16[32,24,1024]{2,1,0:T(8,128)(2,1)} async-done(((bf16[32,24,1024]{2,1,0:T(8,128)(2,1)}), bf16[32,24,1024]{2,1,0:T(8,128)(2,1)}, u32[]{:S(2)}, u32[]{:S(2)}) %all-to-all-start.2) | async-done | bytes 1572896 | tf_op jit(solution)/shard_map/all_to_all | solution.py:106
  58.2 6.6 %all-to-all-start.1 = ((bf16[32,24,1024]{2,1,0:T(8,128)(2,1)}), bf16[32,24,1024]{2,1,0:T(8,128)(2,1)}, u32[]{:S(2)}, u32[]{:S(2)}) async-start(bf16[32,24,1024]{2,1,0:T(8,128)(2,1)} %bitcast.85), calls=%async_computation.1 | async-start | bytes 3145728 | tf_op jit(solution)/shard_map/all_to_all | solution.py:107
  64.8 3.9 %fusion.6 = f32[768,1024]{1,0:T(8,128)S(1)} fusion(bf16[768,1024]{1,0:T(8,128)(2,1)} %bitcast.8, bf16[1,1024,1024]{2,1,0:T(8,128)(2,1)} %param.11), kind=kOutput, calls=%fused_computation.14 | convolution fusion | flops 1610612736 | bytes 6815744 | tf_op jit(solution)/shard_map/dot_general | solution.py:18
  68.7 1.6 copy-done.26
  70.3 5.6 %multiply_convert_fusion = (bf16[768,1024]{1,0:T(8,128)(2,1)}, f32[768,1024]{1,0:T(8,128)}) fusion(f32[768,1024]{1,0:T(8,128)S(1)} %fusion.6, bf16[768,1024]{1,0:T(8,128)(2,1)} %bitcast.8, bf16[1,1024,1024]{2,1,0:T(8,128)(2,1)S(1)} %copy-done), kind=kOutput, calls=%fused_computation.6 | convolution fusion | flops 1615331328 | bytes 11534336 | tf_op jit(solution)/shard_map/dot_general | solution.py:19
  75.9 27.4 %all-to-all-done.1 = bf16[32,24,1024]{2,1,0:T(8,128)(2,1)} async-done(((bf16[32,24,1024]{2,1,0:T(8,128)(2,1)}), bf16[32,24,1024]{2,1,0:T(8,128)(2,1)}, u32[]{:S(2)}, u32[]{:S(2)}) %all-to-all-start.1) | async-done | bytes 1572896 | tf_op jit(solution)/shard_map/all_to_all | solution.py:107
  103.3 4.4 %fusion.1 = bf16[768]{0:T(1024)(128)(2,1)S(1)} fusion(bf16[32,24,1024]{2,1,0:T(8,128)(2,1)} %all-to-all-done.1, bf16[768,1024]{1,0:T(8,128)(2,1)} %get-tuple-element.15, bf16[1,1024,1024]{2,1,0:T(8,128)(2,1)} %param.13), kind=kOutput, calls=%fused_computation.4 | convolution fusion | flops 1612971264 | bytes 5244416 | tf_op jit(solution)/shard_map/dot_general | solution.py:23
  108.4 6.9 %all-to-all-start.4 = ((bf16[32,1,24]{2,1,0:T(2,128)(2,1)}), bf16[32,1,24]{2,1,0:T(2,128)(2,1)S(1)}, u32[]{:S(2)}, u32[]{:S(2)}) async-start(bf16[32,1,24]{2,1,0:T(2,128)(2,1)} %convert_element_type.231), calls=%async_computation.4 | async-start | bytes 32768 | tf_op jit(solution)/shard_map/all_to_all | solution.py:142
  115.4 9.2 %all-to-all-done.4 = bf16[32,1,24]{2,1,0:T(2,128)(2,1)S(1)} async-done(((bf16[32,1,24]{2,1,0:T(2,128)(2,1)}), bf16[32,1,24]{2,1,0:T(2,128)(2,1)S(1)}, u32[]{:S(2)}, u32[]{:S(2)}) %all-to-all-start.4) | async-done | bytes 1568 | tf_op jit(solution)/shard_map/all_to_all | solution.py:142
  126.2 4.1 %all-to-all-start = ((bf16[32,1,24]{2,1,0:T(2,128)(2,1)}), bf16[32,1,24]{2,1,0:T(2,128)(2,1)S(1)}, u32[]{:S(2)}, u32[]{:S(2)}) async-start(bf16[32,1,24]{2,1,0:T(2,128)(2,1)} %convert_element_type.230), calls=%async_computation | async-start | bytes 32768 | tf_op jit(solution)/shard_map/all_to_all | solution.py:108
  130.4 9.3 %all-to-all-done = bf16[32,1,24]{2,1,0:T(2,128)(2,1)S(1)} async-done(((bf16[32,1,24]{2,1,0:T(2,128)(2,1)}), bf16[32,1,24]{2,1,0:T(2,128)(2,1)S(1)}, u32[]{:S(2)}, u32[]{:S(2)}) %all-to-all-start) | async-done | bytes 1568 | tf_op jit(solution)/shard_map/all_to_all | solution.py:108
  139.9 1.8 fusion.2
  143.1 2.7 %fusion = bf16[32,24,1024]{2,1,0:T(8,128)(2,1)S(1)} fusion(bf16[32,24,1024]{2,1,0:T(8,128)(2,1)} %all-to-all-done.1, f32[32,24]{1,0:T(8,128)S(1)} %bitcast.89), kind=kLoop, calls=%fused_computation.3 | loop fusion | flops 2359296 | bytes 3148800 | tf_op jit(solution)/shard_map/convert_element_type | solution.py:117
  146.2 2.7 %multiply_convert_fusion.1 = (bf16[768,1024]{1,0:T(8,128)(2,1)S(1)}, bf16[768,1024]{1,0:T(8,128)(2,1)S(1)}) fusion(f32[768,1024]{1,0:T(8,128)S(1)} %copy-done.27, f32[768,1024]{1,0:T(8,128)S(1)} %copy-done.28, bf16[768,1024]{1,0:T(8,128)(2,1)S(1)} %bitcast.88, bf16[1,1024,1024]{2,1,0:T(8,128)(2,1)S(1)} %copy-done.23), kind=kOutput, calls=%fused_computation.8 | convolution fusion | flops 1620836352 | bytes 13107200 | tf_op jit(solution)/shard_map/dot_general | solution.py:120
  149.0 1.9 convolution_convert_fusion.3
  150.9 1.6 fusion.42
  153.1 1.9 fusion.36
  155.0 1.6 fusion.31
  156.7 1.6 fusion.46
  158.2 1.6 fusion.44
  159.8 1.9 convolution_convert_fusion.4
  161.8 1.7 fusion.38
  163.5 1.9 fusion.4
  166.3 1.7 collective-permute-start.10
  168.7 1.4 collective-permute-start.12
  172.5 2.7 %collective-permute-start.7 = (bf16[256,512]{1,0:T(8,128)(2,1)}, bf16[256,512]{1,0:T(8,128)(2,1)}, u32[]{:S(2)}, u32[]{:S(2)}) collective-permute-start(bf16[256,512]{1,0:T(8,128)(2,1)} %get-tuple-element.12), channel_id=1, source_target_pairs={{0,192},{32,224},{64,0},{96,32},{128,64},{160,96},{192,128},{224,1... | collective-permute-start | bytes 786440 | tf_op jit(solution)/shard_map/ppermute | solution.py:35
  177.5 3.0 %add_convert_fusion = bf16[768,1024]{1,0:T(8,128)(2,1)} fusion(f32[768,1024]{1,0:T(8,128)S(1)} %fusion.4, bf16[768,1024]{1,0:T(8,128)(2,1)S(1)} %get-tuple-element.7, bf16[1,1024,1024]{2,1,0:T(8,128)(2,1)S(1)} %copy-done), kind=kOutput, calls=%fused_computation.7 | convolution fusion | flops 1612185600 | bytes 8388608 | tf_op jit(solution)/shard_map/dot_general | solution.py:130
  180.5 5.8 %all-to-all-start.3 = ((bf16[32,24,1024]{2,1,0:T(8,128)(2,1)}), bf16[32,24,1024]{2,1,0:T(8,128)(2,1)}, u32[]{:S(2)}, u32[]{:S(2)}) async-start(bf16[32,24,1024]{2,1,0:T(8,128)(2,1)} %bitcast.87), calls=%async_computation.3 | async-start | bytes 3145728 | tf_op jit(solution)/shard_map/all_to_all | solution.py:135
  186.3 2.3 fusion.48
  188.6 3.0 %collective-permute-start.2 = (bf16[256,512]{1,0:T(8,128)(2,1)S(1)}, bf16[256,512]{1,0:T(8,128)(2,1)S(1)}, u32[]{:S(2)}, u32[]{:S(2)}) collective-permute-start(bf16[256,512]{1,0:T(8,128)(2,1)S(1)} %copy-done.22), channel_id=1, source_target_pairs={{0,192},{32,224},{64,0},{96,32},{128,64},{160,96},{192,128},{224,1... | collective-permute-start | bytes 786440 | tf_op jit(solution)/shard_map/ppermute | solution.py:35
  191.6 1.0 fusion.21
  192.9 1.1 fusion.20
  194.1 2.6 %collective-permute-start.13 = (bf16[256,1024]{1,0:T(8,128)(2,1)S(1)}, bf16[256,1024]{1,0:T(8,128)(2,1)S(1)}, u32[]{:S(2)}, u32[]{:S(2)}) collective-permute-start(bf16[256,1024]{1,0:T(8,128)(2,1)S(1)} %pad_maximum_fusion.5), channel_id=1, source_target_pairs={{0,192},{32,224},{64,0},{96,32},{128,64},{160,96},{192,128},{224,1... | collective-permute-start | bytes 1572872 | tf_op jit(solution)/shard_map/ppermute | solution.py:35
  196.7 1.0 fusion.23
  198.0 1.1 fusion.22
  199.2 2.6 %collective-permute-start.8 = (bf16[256,1024]{1,0:T(8,128)(2,1)S(1)}, bf16[256,1024]{1,0:T(8,128)(2,1)S(1)}, u32[]{:S(2)}, u32[]{:S(2)}) collective-permute-start(bf16[256,1024]{1,0:T(8,128)(2,1)S(1)} %pad_maximum_fusion.3), channel_id=1, source_target_pairs={{0,192},{32,224},{64,0},{96,32},{128,64},{160,96},{192,128},{224,1... | collective-permute-start | bytes 1572872 | tf_op jit(solution)/shard_map/ppermute | solution.py:35
  201.8 1.0 fusion.25
  203.2 3.7 %collective-permute-done.11 = bf16[256,1024]{1,0:T(8,128)(2,1)S(1)} collective-permute-done((bf16[256,1024]{1,0:T(8,128)(2,1)S(1)}, bf16[256,1024]{1,0:T(8,128)(2,1)S(1)}, u32[]{:S(2)}, u32[]{:S(2)}) %collective-permute-start.11) | collective-permute-done | bytes 524320 | tf_op jit(solution)/shard_map/ppermute | solution.py:35
  206.9 1.1 collective-permute-done.13
  208.8 9.3 %collective-permute-done.6 = bf16[256,1024]{1,0:T(8,128)(2,1)S(1)} collective-permute-done((bf16[256,1024]{1,0:T(8,128)(2,1)S(1)}, bf16[256,1024]{1,0:T(8,128)(2,1)S(1)}, u32[]{:S(2)}, u32[]{:S(2)}) %collective-permute-start.6) | collective-permute-done | bytes 524320 | tf_op jit(solution)/shard_map/ppermute | solution.py:35
  218.2 1.1 collective-permute-done.8
  220.1 9.2 %collective-permute-done.1 = bf16[256,1024]{1,0:T(8,128)(2,1)S(1)} collective-permute-done((bf16[256,1024]{1,0:T(8,128)(2,1)S(1)}, bf16[256,1024]{1,0:T(8,128)(2,1)S(1)}, u32[]{:S(2)}, u32[]{:S(2)}) %collective-permute-start.1) | collective-permute-done | bytes 524320 | tf_op jit(solution)/shard_map/ppermute | solution.py:35
  229.3 1.2 collective-permute-done.3
  233.5 3.8 %collective-permute-done.4 = bf16[128,1024]{1,0:T(8,128)(2,1)S(1)} collective-permute-done((bf16[128,1024]{1,0:T(8,128)(2,1)S(1)}, bf16[128,1024]{1,0:T(8,128)(2,1)S(1)}, u32[]{:S(2)}, u32[]{:S(2)}) %collective-permute-start.4) | collective-permute-done | bytes 262176 | tf_op jit(solution)/shard_map/ppermute | solution.py:39
  238.2 2.8 %convolution_convert_fusion.5 = bf16[256,1024]{1,0:T(8,128)(2,1)} fusion(bf16[768,1024]{1,0:T(8,128)(2,1)} %bitcast.12, s32[256]{0:T(256)S(1)} %multiply_add_fusion), kind=kOutput, calls=%fused_computation.29 | convolution fusion | flops 403111936 | bytes 2098176 | tf_op jit(solution)/shard_map/dot_general | solution.py:146
  (119 shorter events, 20.4 us)
Async XLA Ops:
  0.6 69.7 %copy-start = (bf16[1,1024,1024]{2,1,0:T(8,128)(2,1)S(1)}, bf16[1,1024,1024]{2,1,0:T(8,128)(2,1)}, u32[]{:S(2)}) copy-start(bf16[1,1024,1024]{2,1,0:T(8,128)(2,1)} %param.12) | copy-start | bytes 6291460
  6.6 12.8 %copy-start.21 = (bf16[256,1024]{1,0:T(8,128)(2,1)S(1)}, bf16[256,1024]{1,0:T(8,128)(2,1)}, u32[]{:S(2)}) copy-start(bf16[256,1024]{1,0:T(8,128)(2,1)} %param.8) | copy-start | bytes 1572868
  6.6 51.6 %all-to-all-start.2 = ((bf16[32,24,1024]{2,1,0:T(8,128)(2,1)}), bf16[32,24,1024]{2,1,0:T(8,128)(2,1)}, u32[]{:S(2)}, u32[]{:S(2)}) async-start(bf16[32,24,1024]{2,1,0:T(8,128)(2,1)} %bitcast.86), calls=%async_computation.2 | async-start | bytes 3145728 | tf_op jit(solution)/shard_map/all_to_all | solution.py:106
  58.2 45.1 %all-to-all-start.1 = ((bf16[32,24,1024]{2,1,0:T(8,128)(2,1)}), bf16[32,24,1024]{2,1,0:T(8,128)(2,1)}, u32[]{:S(2)}, u32[]{:S(2)}) async-start(bf16[32,24,1024]{2,1,0:T(8,128)(2,1)} %bitcast.85), calls=%async_computation.1 | async-start | bytes 3145728 | tf_op jit(solution)/shard_map/all_to_all | solution.py:107
  103.3 12.0 %copy-start.25 = (bf16[256]{0:T(256)(128)(2,1)S(1)}, bf16[256]{0:T(256)(128)(2,1)}, u32[]{:S(2)}) copy-start(bf16[256]{0:T(256)(128)(2,1)} %param.9) | copy-start | bytes 1540
  108.4 16.2 %all-to-all-start.4 = ((bf16[32,1,24]{2,1,0:T(2,128)(2,1)}), bf16[32,1,24]{2,1,0:T(2,128)(2,1)S(1)}, u32[]{:S(2)}, u32[]{:S(2)}) async-start(bf16[32,1,24]{2,1,0:T(2,128)(2,1)} %convert_element_type.231), calls=%async_computation.4 | async-start | bytes 32768 | tf_op jit(solution)/shard_map/all_to_all | solution.py:142
  126.2 13.5 %all-to-all-start = ((bf16[32,1,24]{2,1,0:T(2,128)(2,1)}), bf16[32,1,24]{2,1,0:T(2,128)(2,1)S(1)}, u32[]{:S(2)}, u32[]{:S(2)}) async-start(bf16[32,1,24]{2,1,0:T(2,128)(2,1)} %convert_element_type.230), calls=%async_computation | async-start | bytes 32768 | tf_op jit(solution)/shard_map/all_to_all | solution.py:108
  139.9 1.9 copy-start.15
  141.8 4.0 %copy-start.28 = (f32[768,1024]{1,0:T(8,128)S(1)}, f32[768,1024]{1,0:T(8,128)}, u32[]{:S(2)}) copy-start(f32[768,1024]{1,0:T(8,128)} %get-tuple-element.16) | copy-start | bytes 9437188
  142.4 3.4 %copy-start.27 = (f32[768,1024]{1,0:T(8,128)S(1)}, f32[768,1024]{1,0:T(8,128)}, u32[]{:S(2)}) copy-start(f32[768,1024]{1,0:T(8,128)} %copy-done.26) | copy-start | bytes 9437188
  143.0 25.0 %copy-start.13 = (f32[256,1024]{1,0:T(8,128)}, f32[256,1024]{1,0:T(8,128)S(1)}, u32[]{:S(2)}) copy-start(f32[256,1024]{1,0:T(8,128)S(1)} %fusion.29) | copy-start | bytes 3145732
  143.1 3.2 %copy-start.23 = (bf16[1,1024,1024]{2,1,0:T(8,128)(2,1)S(1)}, bf16[1,1024,1024]{2,1,0:T(8,128)(2,1)}, u32[]{:S(2)}) copy-start(bf16[1,1024,1024]{2,1,0:T(8,128)(2,1)} %param.13) | copy-start | bytes 6291460
  149.0 14.6 %copy-start.1 = (bf16[768,1024]{1,0:T(8,128)(2,1)}, bf16[768,1024]{1,0:T(8,128)(2,1)S(1)}, u32[]{:S(2)}) copy-start(bf16[768,1024]{1,0:T(8,128)(2,1)S(1)} %get-tuple-element.8) | copy-start | bytes 4718596
  152.5 19.3 %copy-start.11 = (f32[256,1024]{1,0:T(8,128)}, f32[256,1024]{1,0:T(8,128)S(1)}, u32[]{:S(2)}) copy-start(f32[256,1024]{1,0:T(8,128)S(1)} %fusion.42) | copy-start | bytes 3145732
  153.1 17.1 %copy-start.7 = (f32[256,1024]{1,0:T(8,128)}, f32[256,1024]{1,0:T(8,128)S(1)}, u32[]{:S(2)}) copy-start(f32[256,1024]{1,0:T(8,128)S(1)} %fusion.26) | copy-start | bytes 3145732
  155.0 20.1 %copy-start.5 = (f32[256,1024]{1,0:T(8,128)}, f32[256,1024]{1,0:T(8,128)S(1)}, u32[]{:S(2)}) copy-start(f32[256,1024]{1,0:T(8,128)S(1)} %fusion.36) | copy-start | bytes 3145732
  159.8 16.9 %copy-start.9 = (f32[256,1024]{1,0:T(8,128)}, f32[256,1024]{1,0:T(8,128)S(1)}, u32[]{:S(2)}) copy-start(f32[256,1024]{1,0:T(8,128)S(1)} %fusion.44) | copy-start | bytes 3145732
  161.8 1.8 copy-start.24
  163.5 13.9 %copy-start.3 = (f32[256,1024]{1,0:T(8,128)}, f32[256,1024]{1,0:T(8,128)S(1)}, u32[]{:S(2)}) copy-start(f32[256,1024]{1,0:T(8,128)S(1)} %fusion.38) | copy-start | bytes 3145732
  166.3 22.3 %collective-permute-start.10 = (bf16[256,512]{1,0:T(8,128)(2,1)}, bf16[256,512]{1,0:T(8,128)(2,1)}, u32[]{:S(2)}, u32[]{:S(2)}) collective-permute-start(bf16[256,512]{1,0:T(8,128)(2,1)} %get-tuple-element.9), channel_id=1, source_target_pairs={{0,64},{32,96},{64,128},{96,160},{128,192},{160,224},{192,0},{224,... | collective-permute-start | bytes 786440 | tf_op jit(solution)/shard_map/ppermute | solution.py:35
  168.7 24.1 %collective-permute-start.12 = (bf16[256,512]{1,0:T(8,128)(2,1)}, bf16[256,512]{1,0:T(8,128)(2,1)}, u32[]{:S(2)}, u32[]{:S(2)}) collective-permute-start(bf16[256,512]{1,0:T(8,128)(2,1)} %get-tuple-element.10), channel_id=1, source_target_pairs={{0,192},{32,224},{64,0},{96,32},{128,64},{160,96},{192,128},{224,1... | collective-permute-start | bytes 786440 | tf_op jit(solution)/shard_map/ppermute | solution.py:35
  171.7 22.4 %collective-permute-start.5 = (bf16[256,512]{1,0:T(8,128)(2,1)}, bf16[256,512]{1,0:T(8,128)(2,1)}, u32[]{:S(2)}, u32[]{:S(2)}) collective-permute-start(bf16[256,512]{1,0:T(8,128)(2,1)} %get-tuple-element.11), channel_id=1, source_target_pairs={{0,64},{32,96},{64,128},{96,160},{128,192},{160,224},{192,0},{224,... | collective-permute-start | bytes 786440 | tf_op jit(solution)/shard_map/ppermute | solution.py:35
  172.5 25.4 %collective-permute-start.7 = (bf16[256,512]{1,0:T(8,128)(2,1)}, bf16[256,512]{1,0:T(8,128)(2,1)}, u32[]{:S(2)}, u32[]{:S(2)}) collective-permute-start(bf16[256,512]{1,0:T(8,128)(2,1)} %get-tuple-element.12), channel_id=1, source_target_pairs={{0,192},{32,224},{64,0},{96,32},{128,64},{160,96},{192,128},{224,1... | collective-permute-start | bytes 786440 | tf_op jit(solution)/shard_map/ppermute | solution.py:35
  176.7 22.5 %collective-permute-start = (bf16[256,512]{1,0:T(8,128)(2,1)}, bf16[256,512]{1,0:T(8,128)(2,1)}, u32[]{:S(2)}, u32[]{:S(2)}) collective-permute-start(bf16[256,512]{1,0:T(8,128)(2,1)} %get-tuple-element.13), channel_id=1, source_target_pairs={{0,64},{32,96},{64,128},{96,160},{128,192},{160,224},{192,0},{224,... | collective-permute-start | bytes 786440 | tf_op jit(solution)/shard_map/ppermute | solution.py:35
  180.5 57.7 %all-to-all-start.3 = ((bf16[32,24,1024]{2,1,0:T(8,128)(2,1)}), bf16[32,24,1024]{2,1,0:T(8,128)(2,1)}, u32[]{:S(2)}, u32[]{:S(2)}) async-start(bf16[32,24,1024]{2,1,0:T(8,128)(2,1)} %bitcast.87), calls=%async_computation.3 | async-start | bytes 3145728 | tf_op jit(solution)/shard_map/all_to_all | solution.py:135
  186.3 2.3 copy-start.22
  186.3 5.4 %copy-start.14 = (f32[256,1024]{1,0:T(8,128)S(1)}, f32[256,1024]{1,0:T(8,128)}, u32[]{:S(2)}) copy-start(f32[256,1024]{1,0:T(8,128)} %copy-done.13) | copy-start | bytes 3145732
  186.3 6.4 %copy-start.20 = (bf16[256,512]{1,0:T(8,128)(2,1)S(1)}, bf16[256,512]{1,0:T(8,128)(2,1)}, u32[]{:S(2)}) copy-start(bf16[256,512]{1,0:T(8,128)(2,1)} %slice.131) | copy-start | bytes 786436
  188.6 4.3 %copy-start.8 = (f32[256,1024]{1,0:T(8,128)S(1)}, f32[256,1024]{1,0:T(8,128)}, u32[]{:S(2)}) copy-start(f32[256,1024]{1,0:T(8,128)} %copy-done.7) | copy-start | bytes 3145732
  188.6 5.4 %copy-start.19 = (bf16[256,512]{1,0:T(8,128)(2,1)S(1)}, bf16[256,512]{1,0:T(8,128)(2,1)}, u32[]{:S(2)}) copy-start(bf16[256,512]{1,0:T(8,128)(2,1)} %slice.130) | copy-start | bytes 786436
  188.6 14.3 %collective-permute-start.2 = (bf16[256,512]{1,0:T(8,128)(2,1)S(1)}, bf16[256,512]{1,0:T(8,128)(2,1)S(1)}, u32[]{:S(2)}, u32[]{:S(2)}) collective-permute-start(bf16[256,512]{1,0:T(8,128)(2,1)S(1)} %copy-done.22), channel_id=1, source_target_pairs={{0,192},{32,224},{64,0},{96,32},{128,64},{160,96},{192,128},{224,1... | collective-permute-start | bytes 786440 | tf_op jit(solution)/shard_map/ppermute | solution.py:35
  192.7 4.1 %copy-start.12 = (f32[256,1024]{1,0:T(8,128)S(1)}, f32[256,1024]{1,0:T(8,128)}, u32[]{:S(2)}) copy-start(f32[256,1024]{1,0:T(8,128)} %copy-done.11) | copy-start | bytes 3145732
  192.7 5.0 %copy-start.18 = (bf16[256,512]{1,0:T(8,128)(2,1)S(1)}, bf16[256,512]{1,0:T(8,128)(2,1)}, u32[]{:S(2)}) copy-start(bf16[256,512]{1,0:T(8,128)(2,1)} %slice.133) | copy-start | bytes 786436
  192.8 14.2 %collective-permute-start.11 = (bf16[256,1024]{1,0:T(8,128)(2,1)S(1)}, bf16[256,1024]{1,0:T(8,128)(2,1)S(1)}, u32[]{:S(2)}, u32[]{:S(2)}) collective-permute-start(bf16[256,1024]{1,0:T(8,128)(2,1)S(1)} %pad_maximum_fusion.4), channel_id=1, source_target_pairs={{0,64},{32,96},{64,128},{96,160},{128,192},{160,224},{192,0},{224,... | collective-permute-start | bytes 1572872 | tf_op jit(solution)/shard_map/ppermute | solution.py:35
  194.0 4.0 %copy-start.6 = (f32[256,1024]{1,0:T(8,128)S(1)}, f32[256,1024]{1,0:T(8,128)}, u32[]{:S(2)}) copy-start(f32[256,1024]{1,0:T(8,128)} %copy-done.5) | copy-start | bytes 3145732
  194.1 5.0 %copy-start.17 = (bf16[256,512]{1,0:T(8,128)(2,1)S(1)}, bf16[256,512]{1,0:T(8,128)(2,1)}, u32[]{:S(2)}) copy-start(bf16[256,512]{1,0:T(8,128)(2,1)} %slice.132) | copy-start | bytes 786436
  194.1 13.9 %collective-permute-start.13 = (bf16[256,1024]{1,0:T(8,128)(2,1)S(1)}, bf16[256,1024]{1,0:T(8,128)(2,1)S(1)}, u32[]{:S(2)}, u32[]{:S(2)}) collective-permute-start(bf16[256,1024]{1,0:T(8,128)(2,1)S(1)} %pad_maximum_fusion.5), channel_id=1, source_target_pairs={{0,192},{32,224},{64,0},{96,32},{128,64},{160,96},{192,128},{224,1... | collective-permute-start | bytes 1572872 | tf_op jit(solution)/shard_map/ppermute | solution.py:35
  197.8 4.1 %copy-start.10 = (f32[256,1024]{1,0:T(8,128)S(1)}, f32[256,1024]{1,0:T(8,128)}, u32[]{:S(2)}) copy-start(f32[256,1024]{1,0:T(8,128)} %copy-done.9) | copy-start | bytes 3145732
  197.8 5.0 %copy-start.16 = (bf16[256,512]{1,0:T(8,128)(2,1)S(1)}, bf16[256,512]{1,0:T(8,128)(2,1)}, u32[]{:S(2)}) copy-start(bf16[256,512]{1,0:T(8,128)(2,1)} %slice.135) | copy-start | bytes 786436
  197.9 20.3 %collective-permute-start.6 = (bf16[256,1024]{1,0:T(8,128)(2,1)S(1)}, bf16[256,1024]{1,0:T(8,128)(2,1)S(1)}, u32[]{:S(2)}, u32[]{:S(2)}) collective-permute-start(bf16[256,1024]{1,0:T(8,128)(2,1)S(1)} %pad_maximum_fusion.2), channel_id=1, source_target_pairs={{0,64},{32,96},{64,128},{96,160},{128,192},{160,224},{192,0},{224,... | collective-permute-start | bytes 1572872 | tf_op jit(solution)/shard_map/ppermute | solution.py:35
  199.1 3.9 %copy-start.4 = (f32[256,1024]{1,0:T(8,128)S(1)}, f32[256,1024]{1,0:T(8,128)}, u32[]{:S(2)}) copy-start(f32[256,1024]{1,0:T(8,128)} %copy-done.3) | copy-start | bytes 3145732
  199.2 20.1 %collective-permute-start.8 = (bf16[256,1024]{1,0:T(8,128)(2,1)S(1)}, bf16[256,1024]{1,0:T(8,128)(2,1)S(1)}, u32[]{:S(2)}, u32[]{:S(2)}) collective-permute-start(bf16[256,1024]{1,0:T(8,128)(2,1)S(1)} %pad_maximum_fusion.3), channel_id=1, source_target_pairs={{0,192},{32,224},{64,0},{96,32},{128,64},{160,96},{192,128},{224,1... | collective-permute-start | bytes 1572872 | tf_op jit(solution)/shard_map/ppermute | solution.py:35
  202.9 5.2 %copy-start.2 = (f32[256,1024]{1,0:T(8,128)S(1)}, f32[256,1024]{1,0:T(8,128)}, u32[]{:S(2)}) copy-start(f32[256,1024]{1,0:T(8,128)} %fusion.31) | copy-start | bytes 3145732
  202.9 26.4 %collective-permute-start.1 = (bf16[256,1024]{1,0:T(8,128)(2,1)S(1)}, bf16[256,1024]{1,0:T(8,128)(2,1)S(1)}, u32[]{:S(2)}, u32[]{:S(2)}) collective-permute-start(bf16[256,1024]{1,0:T(8,128)(2,1)S(1)} %pad_maximum_fusion), channel_id=1, source_target_pairs={{0,64},{32,96},{64,128},{96,160},{128,192},{160,224},{192,0},{224,... | collective-permute-start | bytes 1572872 | tf_op jit(solution)/shard_map/ppermute | solution.py:35
  206.9 23.6 %collective-permute-start.3 = (bf16[256,1024]{1,0:T(8,128)(2,1)S(1)}, bf16[256,1024]{1,0:T(8,128)(2,1)S(1)}, u32[]{:S(2)}, u32[]{:S(2)}) collective-permute-start(bf16[256,1024]{1,0:T(8,128)(2,1)S(1)} %pad_maximum_fusion.1), channel_id=1, source_target_pairs={{0,192},{32,224},{64,0},{96,32},{128,64},{160,96},{192,128},{224,1... | collective-permute-start | bytes 1572872 | tf_op jit(solution)/shard_map/ppermute | solution.py:35
  208.3 23.0 %collective-permute-start.14 = (bf16[128,1024]{1,0:T(8,128)(2,1)S(1)}, bf16[128,1024]{1,0:T(8,128)(2,1)S(1)}, u32[]{:S(2)}, u32[]{:S(2)}) collective-permute-start(bf16[128,1024]{1,0:T(8,128)(2,1)S(1)} %dynamic-slice_convert_fusion), channel_id=1, source_target_pairs={{0,32},{32,0},{64,96},{96,64},{128,160},{160,128},{192,224},{224,1... | collective-permute-start | bytes 786440 | tf_op jit(solution)/shard_map/ppermute | solution.py:39
  219.5 13.1 %collective-permute-start.9 = (bf16[128,1024]{1,0:T(8,128)(2,1)S(1)}, bf16[128,1024]{1,0:T(8,128)(2,1)S(1)}, u32[]{:S(2)}, u32[]{:S(2)}) collective-permute-start(bf16[128,1024]{1,0:T(8,128)(2,1)S(1)} %dynamic-slice_convert_fusion.1), channel_id=1, source_target_pairs={{0,32},{32,0},{64,96},{96,64},{128,160},{160,128},{192,224},{224,1... | collective-permute-start | bytes 786440 | tf_op jit(solution)/shard_map/ppermute | solution.py:39
  230.8 6.5 %collective-permute-start.4 = (bf16[128,1024]{1,0:T(8,128)(2,1)S(1)}, bf16[128,1024]{1,0:T(8,128)(2,1)S(1)}, u32[]{:S(2)}, u32[]{:S(2)}) collective-permute-start(bf16[128,1024]{1,0:T(8,128)(2,1)S(1)} %dynamic-slice_convert_fusion.2), channel_id=1, source_target_pairs={{0,32},{32,0},{64,96},{96,64},{128,160},{160,128},{192,224},{224,1... | collective-permute-start | bytes 786440 | tf_op jit(solution)/shard_map/ppermute | solution.py:39
  (1 other events, 1.6 us)

commit v2 on v0

v2 whole, which is shorter than its diff:
```python
import jax
import jax.numpy as jnp
from jax import lax
from jax.sharding import PartitionSpec as P


def shift_y(value, step):
    pairs = []
    for dp in range(8):
        y, low = divmod(dp, 2)
        pairs.append((dp, ((y + step) % 4) * 2 + low))
    return lax.ppermute(value, "dp", pairs)


def swap_low(value):
    return lax.ppermute(value, "dp", [(dp, dp ^ 1) for dp in range(8)])


def chunk(pair, y, offset):
    left, right = pair
    start = ((y + offset) % 4) * 256
    piece = lax.dynamic_slice_in_dim(left, start, 256, axis=1)
    return lax.dot_general(
        piece, right, (((0,), (0,)), ((), ())), preferred_element_type=jnp.float32
    )


HALF = 512


def far_part(pair):
    return chunk(pair, lax.axis_index("dp") // 2, 2).astype(jnp.bfloat16)


def first_step(far):
    return shift_y(far[:, :HALF], 1), shift_y(far[:, HALF:], -1)


def second_values(pair, got):
    y = lax.axis_index("dp") // 2
    from_left, from_right = got
    up_part = chunk(pair, y, 1)
    down_part = chunk(pair, y, 3)
    up_part = jnp.concatenate(
        [up_part[:, :HALF] + from_left.astype(jnp.float32), up_part[:, HALF:]], axis=1
    )
    down_part = jnp.concatenate(
        [down_part[:, :HALF], down_part[:, HALF:] + from_right.astype(jnp.float32)], axis=1
    )
    return up_part.astype(jnp.bfloat16), down_part.astype(jnp.bfloat16)


def second_step(values):
    return shift_y(values[0], 1), shift_y(values[1], -1)


def third_values(pair, got):
    index = lax.axis_index("dp")
    low = index % 2
    total = chunk(pair, index // 2, 0) + got[0].astype(jnp.float32) + got[1].astype(jnp.float32)
    away = lax.dynamic_slice_in_dim(total, (1 - low) * 128, 128, axis=0)
    keep = lax.dynamic_slice_in_dim(total, low * 128, 128, axis=0)
    return keep, away.astype(jnp.bfloat16)


def third_step(values):
    return (values[0] + swap_low(values[1]).astype(jnp.float32))[None]


def summed_part(pair):
    got = first_step(far_part(pair))
    got = second_step(second_values(pair, got))
    return third_step(third_values(pair, got))


def after(values, *others):
    return lax.optimization_barrier((values, others))[0]


def turned(a, b):
    return lax.dot_general(a, b, (((1,), (1,)), ((), ())), preferred_element_type=jnp.float32)


def gated(rows_in, gate_weight, up_weight):
    gate = jnp.dot(rows_in, gate_weight, preferred_element_type=jnp.float32)
    up = jnp.dot(rows_in, up_weight, preferred_element_type=jnp.float32)
    return gate, up


def factors(gate, up):
    sigmoid_gate = jax.nn.sigmoid(gate)
    activation = gate * sigmoid_gate
    hidden = (activation * up).astype(jnp.bfloat16)
    slope = up * sigmoid_gate * (1.0 + gate * (1.0 - sigmoid_gate))
    return hidden, activation, slope


def expert_back(grad_hidden, hidden, activation, slope):
    grad_gate_pre = (grad_hidden * slope).astype(jnp.bfloat16)
    grad_up_pre = (grad_hidden * activation).astype(jnp.bfloat16)
    moved = jnp.sum(hidden.astype(jnp.float32) * grad_hidden, axis=1)
    return grad_gate_pre, grad_up_pre, moved


CAPACITY = 24
NOTES = 128


def exchange(value):
    devices = lax.axis_size("expert")
    blocks = value.reshape(devices, CAPACITY, value.shape[1])
    blocks = lax.all_to_all(blocks, "expert", split_axis=0, concat_axis=0, tiled=True)
    return blocks.reshape(value.shape)


def local(tokens, cotangent, prob, assign, w_gate, w_up, w_down):
    gate_weight, up_weight, down_weight = w_gate[0], w_up[0], w_down[0]
    count, width = tokens.shape
    slots = lax.axis_size("expert") * CAPACITY
    named = assign[:, 0]
    order = jnp.arange(count, dtype=jnp.int32)
    same = (order[:, None] < order[None, :]) & (assign == named[None, :])
    slot = named * CAPACITY + jnp.sum(same.astype(jnp.int32), axis=0)
    pick = (jnp.arange(slots, dtype=jnp.int32)[:, None] == slot[None, :]).astype(jnp.bfloat16)
    scaled = (prob.astype(jnp.float32)[:, None] * cotangent.astype(jnp.float32)).astype(
        jnp.bfloat16
    )

    def gather(value):
        return jnp.dot(pick, value, preferred_element_type=jnp.float32).astype(jnp.bfloat16)

    rows_in = exchange(gather(tokens))
    scaled_in = exchange(after(gather(scaled), rows_in))
    hidden, activation, slope = lax.optimization_barrier(
        factors(*gated(rows_in, gate_weight, up_weight))
    )
    far_down = far_part((hidden, scaled_in))
    first_down = first_step(far_down)
    grad_hidden = turned(scaled_in, down_weight)
    grad_gate_pre, grad_up_pre, moved = expert_back(grad_hidden, hidden, activation, slope)
    far_gate = far_part((rows_in, grad_gate_pre))
    far_up = far_part((rows_in, grad_up_pre))
    first_gate = first_step(far_gate)
    first_up = first_step(far_up)
    grad_gate_pre, grad_up_pre = after((grad_gate_pre, grad_up_pre), far_gate, far_up)
    grad_rows = (turned(grad_gate_pre, gate_weight) + turned(grad_up_pre, up_weight)).astype(
        jnp.bfloat16
    )
    notes = jnp.broadcast_to(moved.astype(jnp.bfloat16)[:, None], (slots, NOTES))
    leaving = after(jnp.concatenate([grad_rows, notes], axis=1), first_down)
    home = exchange(leaving)
    pairs = ((hidden, scaled_in), (rows_in, grad_gate_pre), (rows_in, grad_up_pre))
    pairs = after(pairs, leaving)
    parts = []
    for pair, first in zip(pairs, (first_down, first_gate, first_up)):
        second = second_step(second_values(pair, first))
        parts.append(third_step(third_values(pair, second)))
    returned = lax.dot_general(
        pick, home, (((0,), (0,)), ((), ())), preferred_element_type=jnp.float32
    )
    grad_tokens = returned[:, :width].astype(jnp.bfloat16)
    grad_prob = (returned[:, width] / prob.astype(jnp.float32)).astype(jnp.bfloat16)
    return (grad_tokens, grad_prob, parts[1], parts[2], parts[0])


def solution(mesh):
    placed = (
        P(("dp", "expert"), None),
        P(("dp", "expert"), None),
        P(("dp", "expert")),
        P(("dp", "expert"), None),
        P("expert", None, None),
        P("expert", None, None),
        P("expert", None, None),
    )
    return jax.shard_map(
        local,
        mesh=mesh,
        in_specs=placed,
        out_specs=(
            P(("dp", "expert"), None),
            P(("dp", "expert")),
            P("expert", "dp", None),
            P("expert", "dp", None),
            P("expert", "dp", None),
        ),
        check_vma=False,
    )
```

time: 356 us -> 199 us (0.56)
  waiting for transfers between devices: 179 us -> 85.7 us
  blocking collectives: 73.1 us -> 0 us
  starting transfers between devices: 26.2 us -> 46.9 us
  between operations: 13.9 us -> 1.26 us
  matrix products: 45.2 us -> 49.5 us
    reduce_scatter x3 -> x0, waiting for transfers between devices: 105 us -> none  [the longest x1 55.1 us: local(): lax.psum_scatter(part_gate[None].astype(jnp.bfloat16), 'dp', scatter_dime...]
    all_to_all x2 -> x0, blocking collectives: 73.1 us -> none  [the longest x1 60.4 us: local(): lax.all_to_all(grad_rows.reshape(experts, capacity, width), 'expert', spl...]
    ppermute x0 -> x15, waiting for transfers between devices: none -> 21.6 us  [the longest x12 12.8 us: shift_y(): return lax.ppermute(value, 'dp', pairs)]
    ppermute x0 -> x15, starting transfers between devices: none -> 19 us  [the longest x12 15.6 us: shift_y(): return lax.ppermute(value, 'dp', pairs)]
    all_to_all x3, waiting for transfers between devices: 74.2 us -> 64.1 us  [exchange(): lax.all_to_all(blocks, 'expert', split_axis=0, concat_axis=0, tiled=True)]
    convert_element_type x10 -> x2, other arithmetic: 10.1 us -> 0.54 us  [the longest x1 0.53 us: local(): (returned[:, width] / prob.astype(jnp.float32)).astype(jnp.bfloat16)]
    dot_general x12 -> x20, matrix products: 45.2 us -> 49.5 us  [the longest x12 21.5 us: chunk(): lax.dot_general(piece, right, (((0,), (0,)), ((), ())), preferred_element...]
    another operation x2 -> x6, other arithmetic: 0.61 us -> 4.43 us
  transfers between devices with their start and end apart: 6 -> 18, of which waited for: 5 -> 7; matrix products, arithmetic and copies ran while one was open for 11% -> 20% of each run, Pallas kernels for 0% -> 0%
where the time goes in v2:
time: 199 us; the launch traced here: 198 us
  waiting for transfers between devices  85.7 us (43%)
  matrix products  49.5 us (25%)
  starting transfers between devices  46.9 us (24%)
  other arithmetic  11.6 us (6%)
  local copies, waits for them, and re-layouts  2.6 us (1%)
    all_to_all x3, waiting for transfers between devices, exchange(): lax.all_to_all(blocks, 'expert', split_axis=0, concat_axis=0, tiled=True)  64.1 us
    all_to_all x3, starting transfers between devices, exchange(): lax.all_to_all(blocks, 'expert', split_axis=0, concat_axis=0, tiled=True)  27.9 us
    dot_general x12, matrix products, chunk(): lax.dot_general(piece, right, (((0,), (0,)), ((), ())), preferred_element...  21.5 us
    ppermute x12, starting transfers between devices, shift_y(): return lax.ppermute(value, 'dp', pairs)  15.6 us
    ppermute x12, waiting for transfers between devices, shift_y(): return lax.ppermute(value, 'dp', pairs)  12.8 us
    dot_general x3, matrix products, turned(): lax.dot_general(a, b, (((1,), (1,)), ((), ())), preferred_element_type=jn...  9.76 us
    ppermute x3, waiting for transfers between devices, swap_low(): return lax.ppermute(value, 'dp', [(dp, dp ^ 1) for dp in range(8)])  8.84 us
    dot_general x1, matrix products, gated(): gate = jnp.dot(rows_in, gate_weight, preferred_element_type=jnp.float32)  7.35 us
  transfers between devices with their start and end apart: 18, of which 7 were waited for; matrix products, arithmetic and copies ran while one was open for 20% of the time, Pallas kernels for 0%

profile of v2, /device:TPU:1, one launch (start us, length us, event | category | flops | bytes accessed | tf_op | source)
XLA Modules:
  0.0 197.6 jit_solution(8311086384730752855)
XLA Ops:
  0.6 1.0 convert_reduce_fusion
  2.3 2.9 %convolution_convert_fusion = bf16[768,1024]{1,0:T(8,128)(2,1)} fusion(bf16[256,1024]{1,0:T(8,128)(2,1)} %param.7, s32[256]{0:T(256)S(1)} %multiply_add_fusion), kind=kOutput, calls=%fused_computation.19 | convolution fusion | flops 403636224 | bytes 2098176 | tf_op jit(solution)/shard_map/dot_general | solution.py:130
  5.2 12.8 %all-to-all-start = ((bf16[32,24,1024]{2,1,0:T(8,128)(2,1)}), bf16[32,24,1024]{2,1,0:T(8,128)(2,1)}, u32[]{:S(2)}, u32[]{:S(2)}) async-start(bf16[32,24,1024]{2,1,0:T(8,128)(2,1)} %bitcast.52), calls=%async_computation | async-start | bytes 3145728 | tf_op jit(solution)/shard_map/all_to_all | solution.py:112
  18.0 1.8 convolution_convert_fusion.1
  19.8 36.9 %all-to-all-done = bf16[32,24,1024]{2,1,0:T(8,128)(2,1)} async-done(((bf16[32,24,1024]{2,1,0:T(8,128)(2,1)}), bf16[32,24,1024]{2,1,0:T(8,128)(2,1)}, u32[]{:S(2)}, u32[]{:S(2)}) %all-to-all-start) | async-done | bytes 1572896 | tf_op jit(solution)/shard_map/all_to_all | solution.py:112
  56.7 6.6 %all-to-all-start.1 = ((bf16[32,24,1024]{2,1,0:T(8,128)(2,1)}), bf16[32,24,1024]{2,1,0:T(8,128)(2,1)}, u32[]{:S(2)}, u32[]{:S(2)}) async-start(bf16[32,24,1024]{2,1,0:T(8,128)(2,1)} %bitcast.51), calls=%async_computation.1 | async-start | bytes 3145728 | tf_op jit(solution)/shard_map/all_to_all | solution.py:112
  63.5 3.9 %fusion.3 = f32[768,1024]{1,0:T(8,128)S(1)} fusion(bf16[768,1024]{1,0:T(8,128)(2,1)} %bitcast.2, bf16[1,1024,1024]{2,1,0:T(8,128)(2,1)} %param.12), kind=kOutput, calls=%fused_computation.10 | convolution fusion | flops 1610612736 | bytes 6815744 | tf_op jit(solution)/shard_map/dot_general | solution.py:86
  67.4 7.3 %add_multiply_fusion = (f32[768,1024]{1,0:T(8,128)}, bf16[768,1024]{1,0:T(8,128)(2,1)}, f32[768,1024]{1,0:T(8,128)}) fusion(f32[768,1024]{1,0:T(8,128)S(1)} %fusion.3, bf16[768,1024]{1,0:T(8,128)(2,1)} %bitcast.2, bf16[1,1024,1024]{2,1,0:T(8,128)(2,1)S(1)} %copy-done), kind=kOutput, calls=%fused_computation.4 | convolution fusion | flops 1619263488 | bytes 14680064 | tf_op jit(solution)/shard_map/dot_general | solution.py:85
  74.7 27.2 %all-to-all-done.1 = bf16[32,24,1024]{2,1,0:T(8,128)(2,1)} async-done(((bf16[32,24,1024]{2,1,0:T(8,128)(2,1)}), bf16[32,24,1024]{2,1,0:T(8,128)(2,1)}, u32[]{:S(2)}, u32[]{:S(2)}) %all-to-all-start.1) | async-done | bytes 1572896 | tf_op jit(solution)/shard_map/all_to_all | solution.py:112
  101.9 2.3 %convolution_convert_fusion.2 = bf16[256,1024]{1,0:T(8,128)(2,1)S(1)} fusion(bf16[768,1024]{1,0:T(8,128)(2,1)} %bitcast.4, bf16[768,1024]{1,0:T(8,128)(2,1)} %get-tuple-element.29, s32[]{:T(128)S(6)} %select_n.87), kind=kOutput, calls=%fused_computation.21 | convolution fusion | flops 402915328 | bytes 2490372 | tf_op jit(solution)/shard_map/dot_general | solution.py:23
  104.2 6.1 %multiply_convert_fusion = (bf16[768,1024]{1,0:T(8,128)(2,1)S(1)}, bf16[768]{0:T(1024)(128)(2,1)S(1)}, bf16[768,1024]{1,0:T(8,128)(2,1)S(1)}) fusion(f32[768,1024]{1,0:T(8,128)} %get-tuple-element.20, bf16[768,1024]{1,0:T(8,128)(2,1)S(1)} %copy-done.6, f32[768,1024]{1,0:T(8,128)} %get-tuple-element.19, bf16[768,1024]{1,0:T(8,128)(2,1)} %bitcast.4, ...), kind=kOutput, calls=%fused_computation.2 | convolution fusion | flops 1616116992 | bytes 14681600 | tf_op jit(solution)/shard_map/dot_general | solution.py:81
  110.2 1.9 convolution_convert_fusion.4
  112.2 1.7 convolution_convert_fusion.3
  114.7 1.8 fusion.1
  116.6 1.4 collective-permute-start
  118.0 1.7 collective-permute-start.1
  119.7 1.2 collective-permute-start.4
  121.2 2.4 %collective-permute-start.9 = (bf16[256,512]{1,0:T(8,128)(2,1)S(1)}, bf16[256,512]{1,0:T(8,128)(2,1)}, u32[]{:S(2)}, u32[]{:S(2)}) collective-permute-start(bf16[256,512]{1,0:T(8,128)(2,1)S(1)} %get-tuple-element.38), channel_id=1, source_target_pairs={{0,192},{32,224},{64,0},{96,32},{128,64},{160,96},{192,128},{224,1... | collective-permute-start | bytes 786440 | tf_op jit(solution)/shard_map/ppermute | solution.py:12
  123.6 1.9 add_convert_fusion
  125.6 1.4 pad_maximum_fusion
  127.0 8.5 %all-to-all-start.2 = ((bf16[32,24,1152]{2,1,0:T(8,128)(2,1)}), bf16[32,24,1152]{2,1,0:T(8,128)(2,1)}, u32[]{:S(2)}, u32[]{:S(2)}) async-start(bf16[32,24,1152]{2,1,0:T(8,128)(2,1)} %bitcast.8), calls=%async_computation.2 | async-start | bytes 3538944 | tf_op jit(solution)/shard_map/all_to_all | solution.py:112
  135.6 1.6 fusion.33
  137.2 1.0 fusion.18
  138.3 3.0 %collective-permute-start.5 = (bf16[256,1024]{1,0:T(8,128)(2,1)S(1)}, bf16[256,1024]{1,0:T(8,128)(2,1)S(1)}, u32[]{:S(2)}, u32[]{:S(2)}) collective-permute-start(bf16[256,1024]{1,0:T(8,128)(2,1)S(1)} %pad_maximum_fusion.2), channel_id=1, source_target_pairs={{0,192},{32,224},{64,0},{96,32},{128,64},{160,96},{192,128},{224,1... | collective-permute-start | bytes 1572872 | tf_op jit(solution)/shard_map/ppermute | solution.py:12
  141.3 1.6 fusion.35
  143.0 1.1 fusion.19
  144.4 1.6 fusion.27
  146.0 1.0 fusion.16
  147.1 2.6 %collective-permute-start.10 = (bf16[256,1024]{1,0:T(8,128)(2,1)S(1)}, bf16[256,1024]{1,0:T(8,128)(2,1)S(1)}, u32[]{:S(2)}, u32[]{:S(2)}) collective-permute-start(bf16[256,1024]{1,0:T(8,128)(2,1)S(1)} %pad_maximum_fusion.4), channel_id=1, source_target_pairs={{0,192},{32,224},{64,0},{96,32},{128,64},{160,96},{192,128},{224,1... | collective-permute-start | bytes 1572872 | tf_op jit(solution)/shard_map/ppermute | solution.py:12
  149.7 1.6 fusion.29
  151.4 1.1 fusion.17
  152.8 2.0 %fusion.21 = f32[256,1024]{1,0:T(8,128)S(1)} fusion(bf16[768,1024]{1,0:T(8,128)(2,1)} %bitcast.4, bf16[768,1024]{1,0:T(8,128)(2,1)S(1)} %copy-done.7, s32[]{:T(128)S(6)} %select_n.93), kind=kOutput, calls=%fused_computation.62 | convolution fusion | flops 402653184 | bytes 3014660 | tf_op jit(solution)/shard_map/dot_general | solution.py:23
  155.0 2.8 %collective-permute-start.13 = (bf16[256,1024]{1,0:T(8,128)(2,1)S(1)}, bf16[256,1024]{1,0:T(8,128)(2,1)S(1)}, u32[]{:S(2)}, u32[]{:S(2)}) collective-permute-start(bf16[256,1024]{1,0:T(8,128)(2,1)S(1)} %pad_maximum_fusion.6), channel_id=1, source_target_pairs={{0,192},{32,224},{64,0},{96,32},{128,64},{160,96},{192,128},{224,1... | collective-permute-start | bytes 1572872 | tf_op jit(solution)/shard_map/ppermute | solution.py:12
  157.8 1.6 fusion.37
  159.4 1.6 fusion.31
  161.0 2.0 %fusion.23 = f32[256,1024]{1,0:T(8,128)S(1)} fusion(bf16[768,1024]{1,0:T(8,128)(2,1)} %bitcast.4, bf16[768,1024]{1,0:T(8,128)(2,1)S(1)} %copy-done.7, s32[]{:T(128)S(6)} %select_n.91), kind=kOutput, calls=%fused_computation.64 | convolution fusion | flops 402653184 | bytes 3014660 | tf_op jit(solution)/shard_map/dot_general | solution.py:23
  163.2 2.0 %fusion.25 = f32[256,1024]{1,0:T(8,128)S(1)} fusion(bf16[768,1024]{1,0:T(8,128)(2,1)} %bitcast.4, bf16[768,1024]{1,0:T(8,128)(2,1)S(1)} %copy-done.7, s32[]{:T(128)S(6)} %select_n.89), kind=kOutput, calls=%fused_computation.66 | convolution fusion | flops 402653184 | bytes 3014660 | tf_op jit(solution)/shard_map/dot_general | solution.py:23
  165.6 1.2 collective-permute-start.6
  166.9 2.8 %collective-permute-done.8 = bf16[256,1024]{1,0:T(8,128)(2,1)S(1)} collective-permute-done((bf16[256,1024]{1,0:T(8,128)(2,1)S(1)}, bf16[256,1024]{1,0:T(8,128)(2,1)S(1)}, u32[]{:S(2)}, u32[]{:S(2)}) %collective-permute-start.8) | collective-permute-done | bytes 524320 | tf_op jit(solution)/shard_map/ppermute | solution.py:12
  170.0 1.0 collective-permute-start.11
  170.9 3.9 %collective-permute-done.13 = bf16[256,1024]{1,0:T(8,128)(2,1)S(1)} collective-permute-done((bf16[256,1024]{1,0:T(8,128)(2,1)S(1)}, bf16[256,1024]{1,0:T(8,128)(2,1)S(1)}, u32[]{:S(2)}, u32[]{:S(2)}) %collective-permute-start.13) | collective-permute-done | bytes 524320 | tf_op jit(solution)/shard_map/ppermute | solution.py:12
  174.8 6.0 %collective-permute-done.12 = bf16[256,1024]{1,0:T(8,128)(2,1)S(1)} collective-permute-done((bf16[256,1024]{1,0:T(8,128)(2,1)S(1)}, bf16[256,1024]{1,0:T(8,128)(2,1)S(1)}, u32[]{:S(2)}, u32[]{:S(2)}) %collective-permute-start.12) | collective-permute-done | bytes 524320 | tf_op jit(solution)/shard_map/ppermute | solution.py:12
  181.1 1.2 collective-permute-start.14
  183.2 4.1 %collective-permute-done.11 = bf16[128,1024]{1,0:T(8,128)(2,1)S(1)} collective-permute-done((bf16[128,1024]{1,0:T(8,128)(2,1)S(1)}, bf16[128,1024]{1,0:T(8,128)(2,1)S(1)}, u32[]{:S(2)}, u32[]{:S(2)}) %collective-permute-start.11) | collective-permute-done | bytes 262176 | tf_op jit(solution)/shard_map/ppermute | solution.py:16
  188.1 4.8 %collective-permute-done.14 = bf16[128,1024]{1,0:T(8,128)(2,1)S(1)} collective-permute-done((bf16[128,1024]{1,0:T(8,128)(2,1)S(1)}, bf16[128,1024]{1,0:T(8,128)(2,1)S(1)}, u32[]{:S(2)}, u32[]{:S(2)}) %collective-permute-start.14) | collective-permute-done | bytes 262176 | tf_op jit(solution)/shard_map/ppermute | solution.py:16
  192.9 0.9 add_bitcast_fusion
  193.7 2.3 %fusion.13 = f32[256,1152]{1,0:T(8,128)S(1)} fusion(bf16[768,1152]{1,0:T(8,128)(2,1)} %bitcast.9, s32[256]{0:T(256)S(1)} %multiply_add_fusion), kind=kOutput, calls=%fused_computation.30 | convolution fusion | flops 453181440 | bytes 2950144 | tf_op jit(solution)/shard_map/dot_general | solution.py:158
  196.1 0.9 slice.133
  (68 shorter events, 6.3 us)
Async XLA Ops:
  0.6 66.7 %copy-start = (bf16[1,1024,1024]{2,1,0:T(8,128)(2,1)S(1)}, bf16[1,1024,1024]{2,1,0:T(8,128)(2,1)}, u32[]{:S(2)}) copy-start(bf16[1,1024,1024]{2,1,0:T(8,128)(2,1)} %param.11) | copy-start | bytes 6291460
  5.2 12.8 %copy-start.9 = (bf16[256]{0:T(256)(128)(2,1)S(1)}, bf16[256]{0:T(256)(128)(2,1)}, u32[]{:S(2)}) copy-start(bf16[256]{0:T(256)(128)(2,1)} %param.9) | copy-start | bytes 1540
  5.2 12.8 %copy-start.8 = (bf16[256,1024]{1,0:T(8,128)(2,1)S(1)}, bf16[256,1024]{1,0:T(8,128)(2,1)}, u32[]{:S(2)}) copy-start(bf16[256,1024]{1,0:T(8,128)(2,1)} %param.8) | copy-start | bytes 1572868
  5.2 51.6 %all-to-all-start = ((bf16[32,24,1024]{2,1,0:T(8,128)(2,1)}), bf16[32,24,1024]{2,1,0:T(8,128)(2,1)}, u32[]{:S(2)}, u32[]{:S(2)}) async-start(bf16[32,24,1024]{2,1,0:T(8,128)(2,1)} %bitcast.52), calls=%async_computation | async-start | bytes 3145728 | tf_op jit(solution)/shard_map/all_to_all | solution.py:112
  56.7 45.1 %all-to-all-start.1 = ((bf16[32,24,1024]{2,1,0:T(8,128)(2,1)}), bf16[32,24,1024]{2,1,0:T(8,128)(2,1)}, u32[]{:S(2)}, u32[]{:S(2)}) async-start(bf16[32,24,1024]{2,1,0:T(8,128)(2,1)} %bitcast.51), calls=%async_computation.1 | async-start | bytes 3145728 | tf_op jit(solution)/shard_map/all_to_all | solution.py:112
  101.9 2.3 %copy-start.6 = (bf16[768,1024]{1,0:T(8,128)(2,1)S(1)}, bf16[768,1024]{1,0:T(8,128)(2,1)}, u32[]{:S(2)}) copy-start(bf16[768,1024]{1,0:T(8,128)(2,1)} %get-tuple-element.29) | copy-start | bytes 4718596
  110.2 4.5 %copy-start.2 = (bf16[768,1024]{1,0:T(8,128)(2,1)}, bf16[768,1024]{1,0:T(8,128)(2,1)S(1)}, u32[]{:S(2)}) copy-start(bf16[768,1024]{1,0:T(8,128)(2,1)S(1)} %get-tuple-element.28) | copy-start | bytes 4718596
  110.2 13.3 %copy-start.4 = (bf16[768,1024]{1,0:T(8,128)(2,1)}, bf16[768,1024]{1,0:T(8,128)(2,1)S(1)}, u32[]{:S(2)}) copy-start(bf16[768,1024]{1,0:T(8,128)(2,1)S(1)} %get-tuple-element.26) | copy-start | bytes 4718596
  112.2 2.6 %copy-start.10 = (bf16[1,1024,1024]{2,1,0:T(8,128)(2,1)S(1)}, bf16[1,1024,1024]{2,1,0:T(8,128)(2,1)}, u32[]{:S(2)}) copy-start(bf16[1,1024,1024]{2,1,0:T(8,128)(2,1)} %param.12) | copy-start | bytes 6291460
  116.6 10.4 %collective-permute-start = (bf16[256,512]{1,0:T(8,128)(2,1)S(1)}, bf16[256,512]{1,0:T(8,128)(2,1)S(1)}, u32[]{:S(2)}, u32[]{:S(2)}) collective-permute-start(bf16[256,512]{1,0:T(8,128)(2,1)S(1)} %get-tuple-element.42), channel_id=1, source_target_pairs={{0,64},{32,96},{64,128},{96,160},{128,192},{160,224},{192,0},{224,... | collective-permute-start | bytes 786440 | tf_op jit(solution)/shard_map/ppermute | solution.py:12
  118.0 9.0 %collective-permute-start.1 = (bf16[256,512]{1,0:T(8,128)(2,1)S(1)}, bf16[256,512]{1,0:T(8,128)(2,1)S(1)}, u32[]{:S(2)}, u32[]{:S(2)}) collective-permute-start(bf16[256,512]{1,0:T(8,128)(2,1)S(1)} %get-tuple-element.41), channel_id=1, source_target_pairs={{0,192},{32,224},{64,0},{96,32},{128,64},{160,96},{192,128},{224,1... | collective-permute-start | bytes 786440 | tf_op jit(solution)/shard_map/ppermute | solution.py:12
  119.7 17.5 %collective-permute-start.4 = (bf16[256,512]{1,0:T(8,128)(2,1)}, bf16[256,512]{1,0:T(8,128)(2,1)}, u32[]{:S(2)}, u32[]{:S(2)}) collective-permute-start(bf16[256,512]{1,0:T(8,128)(2,1)} %get-tuple-element.40), channel_id=1, source_target_pairs={{0,192},{32,224},{64,0},{96,32},{128,64},{160,96},{192,128},{224,1... | collective-permute-start | bytes 786440 | tf_op jit(solution)/shard_map/ppermute | solution.py:12
  120.9 22.1 %collective-permute-start.2 = (bf16[256,512]{1,0:T(8,128)(2,1)S(1)}, bf16[256,512]{1,0:T(8,128)(2,1)}, u32[]{:S(2)}, u32[]{:S(2)}) collective-permute-start(bf16[256,512]{1,0:T(8,128)(2,1)S(1)} %get-tuple-element.39), channel_id=1, source_target_pairs={{0,64},{32,96},{64,128},{96,160},{128,192},{160,224},{192,0},{224,... | collective-permute-start | bytes 786440 | tf_op jit(solution)/shard_map/ppermute | solution.py:12
  121.2 24.9 %collective-permute-start.9 = (bf16[256,512]{1,0:T(8,128)(2,1)S(1)}, bf16[256,512]{1,0:T(8,128)(2,1)}, u32[]{:S(2)}, u32[]{:S(2)}) collective-permute-start(bf16[256,512]{1,0:T(8,128)(2,1)S(1)} %get-tuple-element.38), channel_id=1, source_target_pairs={{0,192},{32,224},{64,0},{96,32},{128,64},{160,96},{192,128},{224,1... | collective-permute-start | bytes 786440 | tf_op jit(solution)/shard_map/ppermute | solution.py:12
  127.0 24.4 %collective-permute-start.7 = (bf16[256,512]{1,0:T(8,128)(2,1)S(1)}, bf16[256,512]{1,0:T(8,128)(2,1)}, u32[]{:S(2)}, u32[]{:S(2)}) collective-permute-start(bf16[256,512]{1,0:T(8,128)(2,1)S(1)} %get-tuple-element.37), channel_id=1, source_target_pairs={{0,64},{32,96},{64,128},{96,160},{128,192},{160,224},{192,0},{224,... | collective-permute-start | bytes 786440 | tf_op jit(solution)/shard_map/ppermute | solution.py:12
  127.0 8.6 %copy-start.5 = (bf16[768,1024]{1,0:T(8,128)(2,1)S(1)}, bf16[768,1024]{1,0:T(8,128)(2,1)}, u32[]{:S(2)}) copy-start(bf16[768,1024]{1,0:T(8,128)(2,1)} %copy-done.4) | copy-start | bytes 4718596
  127.0 66.7 %all-to-all-start.2 = ((bf16[32,24,1152]{2,1,0:T(8,128)(2,1)}), bf16[32,24,1152]{2,1,0:T(8,128)(2,1)}, u32[]{:S(2)}, u32[]{:S(2)}) async-start(bf16[32,24,1152]{2,1,0:T(8,128)(2,1)} %bitcast.8), calls=%async_computation.2 | async-start | bytes 3538944 | tf_op jit(solution)/shard_map/all_to_all | solution.py:112
  138.3 27.0 %collective-permute-start.5 = (bf16[256,1024]{1,0:T(8,128)(2,1)S(1)}, bf16[256,1024]{1,0:T(8,128)(2,1)S(1)}, u32[]{:S(2)}, u32[]{:S(2)}) collective-permute-start(bf16[256,1024]{1,0:T(8,128)(2,1)S(1)} %pad_maximum_fusion.2), channel_id=1, source_target_pairs={{0,192},{32,224},{64,0},{96,32},{128,64},{160,96},{192,128},{224,1... | collective-permute-start | bytes 1572872 | tf_op jit(solution)/shard_map/ppermute | solution.py:12
  142.9 1.5 copy-start.3
  144.2 21.2 %collective-permute-start.3 = (bf16[256,1024]{1,0:T(8,128)(2,1)S(1)}, bf16[256,1024]{1,0:T(8,128)(2,1)S(1)}, u32[]{:S(2)}, u32[]{:S(2)}) collective-permute-start(bf16[256,1024]{1,0:T(8,128)(2,1)S(1)} %pad_maximum_fusion.1), channel_id=1, source_target_pairs={{0,64},{32,96},{64,128},{96,160},{128,192},{160,224},{192,0},{224,... | collective-permute-start | bytes 1572872 | tf_op jit(solution)/shard_map/ppermute | solution.py:12
  147.1 19.7 %collective-permute-start.10 = (bf16[256,1024]{1,0:T(8,128)(2,1)S(1)}, bf16[256,1024]{1,0:T(8,128)(2,1)S(1)}, u32[]{:S(2)}, u32[]{:S(2)}) collective-permute-start(bf16[256,1024]{1,0:T(8,128)(2,1)S(1)} %pad_maximum_fusion.4), channel_id=1, source_target_pairs={{0,192},{32,224},{64,0},{96,32},{128,64},{160,96},{192,128},{224,1... | collective-permute-start | bytes 1572872 | tf_op jit(solution)/shard_map/ppermute | solution.py:12
  151.3 1.5 copy-start.7
  152.6 17.1 %collective-permute-start.8 = (bf16[256,1024]{1,0:T(8,128)(2,1)S(1)}, bf16[256,1024]{1,0:T(8,128)(2,1)S(1)}, u32[]{:S(2)}, u32[]{:S(2)}) collective-permute-start(bf16[256,1024]{1,0:T(8,128)(2,1)S(1)} %pad_maximum_fusion.3), channel_id=1, source_target_pairs={{0,64},{32,96},{64,128},{96,160},{128,192},{160,224},{192,0},{224,... | collective-permute-start | bytes 1572872 | tf_op jit(solution)/shard_map/ppermute | solution.py:12
  155.0 19.8 %collective-permute-start.13 = (bf16[256,1024]{1,0:T(8,128)(2,1)S(1)}, bf16[256,1024]{1,0:T(8,128)(2,1)S(1)}, u32[]{:S(2)}, u32[]{:S(2)}) collective-permute-start(bf16[256,1024]{1,0:T(8,128)(2,1)S(1)} %pad_maximum_fusion.6), channel_id=1, source_target_pairs={{0,192},{32,224},{64,0},{96,32},{128,64},{160,96},{192,128},{224,1... | collective-permute-start | bytes 1572872 | tf_op jit(solution)/shard_map/ppermute | solution.py:12
  165.3 15.5 %collective-permute-start.12 = (bf16[256,1024]{1,0:T(8,128)(2,1)S(1)}, bf16[256,1024]{1,0:T(8,128)(2,1)S(1)}, u32[]{:S(2)}, u32[]{:S(2)}) collective-permute-start(bf16[256,1024]{1,0:T(8,128)(2,1)S(1)} %pad_maximum_fusion.5), channel_id=1, source_target_pairs={{0,64},{32,96},{64,128},{96,160},{128,192},{160,224},{192,0},{224,... | collective-permute-start | bytes 1572872 | tf_op jit(solution)/shard_map/ppermute | solution.py:12
  165.6 16.7 %collective-permute-start.6 = (bf16[128,1024]{1,0:T(8,128)(2,1)S(1)}, bf16[128,1024]{1,0:T(8,128)(2,1)S(1)}, u32[]{:S(2)}, u32[]{:S(2)}) collective-permute-start(bf16[128,1024]{1,0:T(8,128)(2,1)S(1)} %dynamic-slice_convert_fusion.2), channel_id=1, source_target_pairs={{0,32},{32,0},{64,96},{96,64},{128,160},{160,128},{192,224},{224,1... | collective-permute-start | bytes 786440 | tf_op jit(solution)/shard_map/ppermute | solution.py:16
  170.0 17.3 %collective-permute-start.11 = (bf16[128,1024]{1,0:T(8,128)(2,1)S(1)}, bf16[128,1024]{1,0:T(8,128)(2,1)S(1)}, u32[]{:S(2)}, u32[]{:S(2)}) collective-permute-start(bf16[128,1024]{1,0:T(8,128)(2,1)S(1)} %dynamic-slice_convert_fusion.1), channel_id=1, source_target_pairs={{0,32},{32,0},{64,96},{96,64},{128,160},{160,128},{192,224},{224,1... | collective-permute-start | bytes 786440 | tf_op jit(solution)/shard_map/ppermute | solution.py:16
  181.1 11.7 %collective-permute-start.14 = (bf16[128,1024]{1,0:T(8,128)(2,1)S(1)}, bf16[128,1024]{1,0:T(8,128)(2,1)S(1)}, u32[]{:S(2)}, u32[]{:S(2)}) collective-permute-start(bf16[128,1024]{1,0:T(8,128)(2,1)S(1)} %dynamic-slice_convert_fusion), channel_id=1, source_target_pairs={{0,32},{32,0},{64,96},{96,64},{128,160},{160,128},{192,224},{224,1... | collective-permute-start | bytes 786440 | tf_op jit(solution)/shard_map/ppermute | solution.py:16
  193.7 3.9 %copy-start.1 = (bf16[1,1024,1024]{2,1,0:T(8,128)(2,1)S(1)}, bf16[1,1024,1024]{2,1,0:T(8,128)(2,1)}, u32[]{:S(2)}) copy-start(bf16[1,1024,1024]{2,1,0:T(8,128)(2,1)} %param.11) | copy-start | bytes 6291460

commit v3 on v2

v3 whole, which is shorter than its diff:
```python
import jax
import jax.numpy as jnp
from jax import lax
from jax.experimental import pallas as pl
from jax.experimental.pallas import tpu as pltpu
from jax.sharding import PartitionSpec as P


def shift_y(value, step):
    pairs = []
    for dp in range(8):
        y, low = divmod(dp, 2)
        pairs.append((dp, ((y + step) % 4) * 2 + low))
    return lax.ppermute(value, "dp", pairs)


def swap_low(value):
    return lax.ppermute(value, "dp", [(dp, dp ^ 1) for dp in range(8)])


HALF = 512
BLOCK = 256
LEFT_TURNED = (((0,), (0,)), ((), ()))
RIGHT_TURNED = (((1,), (1,)), ((), ()))


def product(left, right, dimensions):
    return lax.dot_general(left, right, dimensions, preferred_element_type=jnp.float32)


def call(kernel, outputs, position, inputs, flops):
    in_vmem = pl.BlockSpec(memory_space=pltpu.VMEM)
    in_smem = pl.BlockSpec(memory_space=pltpu.SMEM)
    moved = sum(v.size * v.dtype.itemsize for v in inputs)
    return pl.pallas_call(
        kernel,
        out_shape=outputs,
        in_specs=[in_smem] + [in_vmem] * len(inputs),
        out_specs=[in_vmem] * len(outputs),
        compiler_params=pltpu.CompilerParams(vmem_limit_bytes=16 * 1024 * 1024),
        cost_estimate=pl.CostEstimate(flops=flops, bytes_accessed=moved, transcendentals=0),
    )(position, *inputs)


def columns_of(ref, y, offset):
    start = pl.multiple_of(((y + offset) % 4) * BLOCK, BLOCK)
    return ref[:, pl.ds(start, BLOCK)]


def expert_kernel(
    position,
    both,
    w_gate,
    w_up,
    w_down,
    leaving,
    far_low,
    far_high,
    ready_up,
    ready_down,
    add_up,
    add_down,
    own,
    hidden,
    gate_pre,
    up_pre,
):
    y = position[0]
    width = w_gate.shape[0]
    moved = jnp.zeros((both.shape[0], 1), jnp.float32)
    for start in range(0, w_gate.shape[1], BLOCK):
        cut = pl.ds(start, BLOCK)
        gate = jnp.dot(both[:, :width], w_gate[:, cut], preferred_element_type=jnp.float32)
        up = jnp.dot(both[:, :width], w_up[:, cut], preferred_element_type=jnp.float32)
        grad_hidden = product(both[:, width:], w_down[cut, :], RIGHT_TURNED)
        sigmoid_gate = jax.nn.sigmoid(gate)
        active = gate * sigmoid_gate
        held = (active * up).astype(jnp.bfloat16)
        hidden[:, cut] = held
        slope = sigmoid_gate * (1.0 + gate * (1.0 - sigmoid_gate))
        gate_pre[:, cut] = (grad_hidden * up * slope).astype(jnp.bfloat16)
        up_pre[:, cut] = (grad_hidden * active).astype(jnp.bfloat16)
        part = held.astype(jnp.float32) * grad_hidden
        moved = moved + jnp.sum(part, axis=1, keepdims=True)

    scaled = both.at[:, width:]
    pairs = ((hidden, scaled), (both, gate_pre), (both, up_pre))
    cuts = [pl.ds(place * BLOCK, BLOCK) for place in range(3)]
    for cut, (left, right) in zip(cuts, pairs):
        far = product(columns_of(left, y, 2), right[...], LEFT_TURNED).astype(jnp.bfloat16)
        far_low[cut, :] = far[:, :HALF]
        far_high[cut, :] = far[:, HALF:]
    leaving[:, width:] = jnp.broadcast_to(moved, (both.shape[0], NOTES)).astype(jnp.bfloat16)
    for start in range(0, width, BLOCK):
        cut = pl.ds(start, BLOCK)
        grad = product(gate_pre[...], w_gate[cut, :], RIGHT_TURNED)
        grad = grad + product(up_pre[...], w_up[cut, :], RIGHT_TURNED)
        leaving[:, cut] = grad.astype(jnp.bfloat16)
    for cut, (left, right) in zip(cuts, pairs):
        own[cut, :] = product(columns_of(left, y, 0), right[...], LEFT_TURNED)
    for cut, (left, right) in zip(cuts, pairs):
        part = product(columns_of(left, y, 1), right[...], LEFT_TURNED)
        add_up[cut, :] = part[:, :HALF]
        ready_up[cut, :] = part[:, HALF:].astype(jnp.bfloat16)
        part = product(columns_of(left, y, 3), right[...], LEFT_TURNED)
        add_down[cut, :] = part[:, HALF:]
        ready_down[cut, :] = part[:, :HALF].astype(jnp.bfloat16)


def expert(position, both, w_gate, w_up, w_down):
    slots, width = both.shape[0], w_gate.shape[0]
    size = w_gate.shape[1]
    shapes = [((slots, width + NOTES), jnp.bfloat16)]
    shapes += [((3 * BLOCK, HALF), jnp.bfloat16)] * 4
    shapes += [((3 * BLOCK, HALF), jnp.float32)] * 2
    shapes += [((3 * BLOCK, width), jnp.float32)]
    in_vmem = pl.BlockSpec(memory_space=pltpu.VMEM)
    return pl.pallas_call(
        expert_kernel,
        out_shape=[jax.ShapeDtypeStruct(*shape) for shape in shapes],
        in_specs=[pl.BlockSpec(memory_space=pltpu.SMEM)] + [in_vmem] * 4,
        out_specs=[in_vmem] * len(shapes),
        scratch_shapes=[pltpu.VMEM((slots, size), jnp.bfloat16)] * 3,
        compiler_params=pltpu.CompilerParams(vmem_limit_bytes=24 * 1024 * 1024),
        cost_estimate=pl.CostEstimate(
            flops=16 * slots * width * size, bytes_accessed=20_000_000, transcendentals=0
        ),
    )(position, both, w_gate, w_up, w_down)


def pick_of(slot, slots):
    return (lax.broadcasted_iota(jnp.int32, (slots, slot.shape[1]), 0) == slot).astype(
        jnp.bfloat16
    )


def send_kernel(position, named, prob, tokens, cotangent, both, slot):
    count, width = tokens.shape
    square = (count, count)
    across = jnp.broadcast_to(named[...], square)
    earlier = lax.broadcasted_iota(jnp.int32, square, 0) < lax.broadcasted_iota(
        jnp.int32, square, 1
    )
    same = jnp.where(earlier & (across.T == across), 1, 0)
    slot[...] = named[...] * CAPACITY + jnp.sum(same, axis=0, keepdims=True)
    pick = pick_of(slot[...], both.shape[0])
    both[:, :width] = jnp.dot(pick, tokens[...], preferred_element_type=jnp.float32).astype(
        jnp.bfloat16
    )
    weight = jnp.broadcast_to(prob[...], square).T[:, :1]
    scaled = (weight * cotangent[...].astype(jnp.float32)).astype(jnp.bfloat16)
    both[:, width:] = jnp.dot(pick, scaled, preferred_element_type=jnp.float32).astype(
        jnp.bfloat16
    )


def home_kernel(position, slot, prob, home, grad_tokens, grad_prob):
    width = grad_tokens.shape[1]
    pick = pick_of(slot[...], home.shape[0])
    grad_tokens[...] = product(pick, home[:, :width], LEFT_TURNED).astype(jnp.bfloat16)
    moved = product(home[:, width:], pick, LEFT_TURNED)
    grad_prob[...] = moved[:1, :] / prob[...]


def first_step(low, high):
    return shift_y(low, 1), shift_y(high, -1)


def second_values(up_part, down_part, got):
    up_part = (up_part + got[0].astype(jnp.float32)).astype(jnp.bfloat16)
    down_part = (down_part + got[1].astype(jnp.float32)).astype(jnp.bfloat16)
    return lax.optimization_barrier((up_part, down_part))


def third_step(own, ready, added, low):
    left = jnp.concatenate([added[0], ready[0]], axis=1)
    right = jnp.concatenate([ready[1], added[1]], axis=1)
    total = own + left.astype(jnp.float32) + right.astype(jnp.float32)
    away = lax.dynamic_slice_in_dim(total, (1 - low) * 128, 128, axis=0)
    keep = lax.dynamic_slice_in_dim(total, low * 128, 128, axis=0)
    return (keep + swap_low(away.astype(jnp.bfloat16)).astype(jnp.float32))[None]


def after(values, *others):
    return lax.optimization_barrier((values, others))[0]


CAPACITY = 24
NOTES = 128


def exchange(value):
    devices = lax.axis_size("expert")
    blocks = value.reshape(devices, CAPACITY, value.shape[1])
    blocks = lax.all_to_all(blocks, "expert", split_axis=0, concat_axis=0, tiled=True)
    return blocks.reshape(value.shape)


def local(tokens, cotangent, prob, assign, w_gate, w_up, w_down):
    gate_weight, up_weight, down_weight = w_gate[0], w_up[0], w_down[0]
    count, width = tokens.shape
    slots = lax.axis_size("expert") * CAPACITY
    index = lax.axis_index("dp")
    low = index % 2
    position = (index // 2).astype(jnp.int32).reshape(1)
    size = gate_weight.shape[1]
    weight = prob.astype(jnp.float32).reshape(1, count)
    work = 2 * slots * width * size
    both, slot = call(
        send_kernel,
        (
            jax.ShapeDtypeStruct((slots, 2 * width), jnp.bfloat16),
            jax.ShapeDtypeStruct((1, count), jnp.int32),
        ),
        position,
        (assign.reshape(1, count), weight, tokens, cotangent),
        work // 2,
    )
    both = exchange(both)
    leaving, far_low, far_high, ready_up, ready_down, add_up, add_down, own = expert(
        position, both, gate_weight, up_weight, down_weight
    )
    home = exchange(leaving)
    got = lax.optimization_barrier(first_step(far_low, far_high))
    ready = (shift_y(ready_up, 1), shift_y(ready_down, -1))
    cuts = [slice(n * BLOCK, n * BLOCK + BLOCK) for n in range(3)]
    second, values = [], ()
    for cut in cuts:
        values = second_values(
            *after((add_up[cut], add_down[cut]), values), [value[cut] for value in got]
        )
        second.append((shift_y(values[0], 1), shift_y(values[1], -1)))
    parts = []
    for place, (cut, added) in enumerate(zip(cuts, second)):
        mine = after(own[cut], parts[0]) if place == 2 else own[cut]
        parts.append(third_step(mine, [value[cut] for value in ready], added, low))
    grad_tokens, grad_prob = call(
        home_kernel,
        (
            jax.ShapeDtypeStruct((count, width), jnp.bfloat16),
            jax.ShapeDtypeStruct((1, count), jnp.float32),
        ),
        position,
        (slot, weight, home),
        2 * count * slots * width,
    )
    grad_prob = grad_prob.reshape(count).astype(jnp.bfloat16)
    return (grad_tokens, grad_prob, parts[1], parts[2], parts[0])


def solution(mesh):
    placed = (
        P(("dp", "expert"), None),
        P(("dp", "expert"), None),
        P(("dp", "expert")),
        P(("dp", "expert"), None),
        P("expert", None, None),
        P("expert", None, None),
        P("expert", None, None),
    )
    return jax.shard_map(
        local,
        mesh=mesh,
        in_specs=placed,
        out_specs=(
            P(("dp", "expert"), None),
            P(("dp", "expert")),
            P("expert", "dp", None),
            P("expert", "dp", None),
            P("expert", "dp", None),
        ),
        check_vma=False,
    )
```

time: 199 us -> 182 us (0.915)
  blocking collectives: 0 us -> 85.4 us
  waiting for transfers between devices: 85.7 us -> 32.7 us
  matrix products: 49.5 us -> 0 us
  starting transfers between devices: 46.9 us -> 23.9 us
  Pallas kernels: 0 us -> 17.8 us
  local copies, waits for them, and re-layouts: 2.6 us -> 9.54 us
    all_to_all x0 -> x1, blocking collectives: none -> 85.4 us  [exchange(): lax.all_to_all(blocks, 'expert', split_axis=0, concat_axis=0, tiled=True)]
    all_to_all x3 -> x1, waiting for transfers between devices: 64.1 us -> 0.01 us  [exchange(): lax.all_to_all(blocks, 'expert', split_axis=0, concat_axis=0, tiled=True)]
    dot_general x20 -> x0, matrix products: 49.5 us -> none  [the longest x12 21.5 us: chunk(): lax.dot_general(piece, right, (((0,), (0,)), ((), ())), preferred_element...]
    all_to_all x3 -> x1, starting transfers between devices: 27.9 us -> 6.67 us  [exchange(): lax.all_to_all(blocks, 'expert', split_axis=0, concat_axis=0, tiled=True)]
    pallas_call x0 -> x3, Pallas kernels: none -> 17.8 us  [the longest x1 15.3 us: expert(): pl.pallas_call(expert_kernel, out_shape=[jax.ShapeDtypeStruct(*shape) for...]
    ppermute x12 -> x10, waiting for transfers between devices: 12.8 us -> 25.2 us  [shift_y(): return lax.ppermute(value, 'dp', pairs)]
    unnamed x22, local copies, waits for them, and re-layouts: 0.33 us -> 7.4 us
    convert_element_type x2 -> x7, other arithmetic: 0.54 us -> 6.85 us  [the longest x3 3.24 us: second_values(): down_part = (down_part + got[1].astype(jnp.float32)).astype(jnp.bfloat16)]
  transfers between devices with their start and end apart: 18 -> 14, of which waited for: 7 -> 9; matrix products, arithmetic and copies ran while one was open for 20% -> 7% of each run, Pallas kernels for 0% -> 0%
where the time goes in v3:
time: 182 us; the launch traced here: 181 us
  blocking collectives  85.4 us (47%)
  waiting for transfers between devices  32.7 us (18%)
  starting transfers between devices  23.9 us (13%)
  Pallas kernels  17.8 us (10%)
  other arithmetic  10.9 us (6%)
  local copies, waits for them, and re-layouts  9.54 us (5%)
    all_to_all x1, blocking collectives, exchange(): lax.all_to_all(blocks, 'expert', split_axis=0, concat_axis=0, tiled=True)  85.4 us
    ppermute x10, waiting for transfers between devices, shift_y(): return lax.ppermute(value, 'dp', pairs)  25.2 us
    pallas_call x1, Pallas kernels, expert(): pl.pallas_call(expert_kernel, out_shape=[jax.ShapeDtypeStruct(*shape) for...  15.3 us
    ppermute x10, starting transfers between devices, shift_y(): return lax.ppermute(value, 'dp', pairs)  13.7 us
    ppermute x3, waiting for transfers between devices, swap_low(): return lax.ppermute(value, 'dp', [(dp, dp ^ 1) for dp in range(8)])  7.56 us
    unnamed x22, local copies, waits for them, and re-layouts  7.4 us
    all_to_all x1, starting transfers between devices, exchange(): lax.all_to_all(blocks, 'expert', split_axis=0, concat_axis=0, tiled=True)  6.67 us
  transfers between devices with their start and end apart: 14, of which 9 were waited for; matrix products, arithmetic and copies ran while one was open for 7% of the time, Pallas kernels for 0%

profile of v3, /device:TPU:1, one launch (start us, length us, event | category | flops | bytes accessed | tf_op | source)
XLA Modules:
  0.0 181.2 jit_solution(18127016805507807818)
XLA Ops:
  0.6 0.7 reshape.43
  1.3 1.0 copy-done.8
  2.3 1.0 copy-done.9
  3.4 0.7 copy-done.10
  4.1 1.1 shard_map.110
  5.2 85.4 %all_to_all.10 = bf16[32,24,2048]{2,1,0:T(8,128)(2,1)S(1)} all-to-all(bf16[32,24,2048]{2,1,0:T(8,128)(2,1)S(1)} %bitcast.18), channel_id=1, replica_groups=mesh['dp'=8,'expert'=32] {'expert'}, dimensions={0} | all-to-all | bytes 6291456 | tf_op jit(solution)/shard_map/all_to_all | solution.py:195
  90.6 15.3 %shard_map.111 = (bf16[768,1152]{1,0:T(8,128)(2,1)}, bf16[768,512]{1,0:T(8,128)(2,1)}, bf16[768,512]{1,0:T(8,128)(2,1)}, bf16[768,512]{1,0:T(8,128)(2,1)S(1)}, b...) custom-call(s32[1]{0:T(128)} %bitcast.position, ...), custom_call_target="tpu_custom_call" | custom-call | flops 12884901888 | bytes 20000000 | tf_op jit(solution)/shard_map/pallas_call | solution.py:118
  105.9 1.6 copy-done
  107.5 1.2 copy-done.2
  108.7 0.9 copy-done.6
  109.6 0.9 copy-done.7
  110.5 1.5 collective-permute-start
  112.1 1.3 collective-permute-start.1
  113.3 6.7 %all-to-all-start.1 = ((bf16[32,24,1152]{2,1,0:T(8,128)(2,1)}), bf16[32,24,1152]{2,1,0:T(8,128)(2,1)S(1)}, u32[]{:S(2)}, u32[]{:S(2)}) async-start(bf16[32,24,1152]{2,1,0:T(8,128)(2,1)} %bitcast.8), calls=%async_computation.1 | async-start | bytes 3538944 | tf_op jit(solution)/shard_map/all_to_all | solution.py:195
  120.0 0.1 collective-permute-start.3
  120.2 2.6 %collective-permute-start.4 = (bf16[768,512]{1,0:T(8,128)(2,1)}, bf16[768,512]{1,0:T(8,128)(2,1)S(1)}, u32[]{:S(2)}, u32[]{:S(2)}) collective-permute-start(bf16[768,512]{1,0:T(8,128)(2,1)} %copy-done.6), channel_id=1, source_target_pairs={{0,192},{32,224},{64,0},{96,32},{128,64},{160,96},{192,128},{224,1... | collective-permute-start | bytes 2359304 | tf_op jit(solution)/shard_map/ppermute | solution.py:14
  122.8 1.9 %fusion = (f32[256,512]{1,0:T(8,128)S(1)}, f32[256,512]{1,0:T(8,128)S(1)}, f32[256,512]{1,0:T(8,128)S(1)}, f32[256,512]{1,0:T(8,128)S(1)}, f32[256,512]{1,0:T(8,128)S(1)}, /*index=5*/f32[256,512]{1,0:T(8,128)S(1)}) fusion(f32[768,512]{1,0:T(8,128)} %copy-done.2, f32[768,512]{1,0:T(8,128)S(1)} %get-tuple-element.38), kind=kLoop, calls=%fused_computation.16 | loop fusion | bytes 6291456 | tf_op jit(solution)/shard_map/slice | solution.py:230
  124.7 5.3 %collective-permute-done = bf16[768,512]{1,0:T(8,128)(2,1)} collective-permute-done((bf16[768,512]{1,0:T(8,128)(2,1)}, bf16[768,512]{1,0:T(8,128)(2,1)}, u32[]{:S(2)}, u32[]{:S(2)}) %collective-permute-start) | collective-permute-done | bytes 786464 | tf_op jit(solution)/shard_map/ppermute | solution.py:14
  130.0 0.5 collective-permute-done.1
  130.4 1.0 add_convert_fusion.5
  131.5 1.0 add_convert_fusion.4
  132.5 1.3 collective-permute-start.7
  133.8 1.0 add_convert_fusion.3
  134.8 1.0 add_convert_fusion.2
  135.8 0.4 collective-permute-start.2
  136.2 2.4 %collective-permute-start.5 = (bf16[256,512]{1,0:T(8,128)(2,1)S(1)}, bf16[256,512]{1,0:T(8,128)(2,1)S(1)}, u32[]{:S(2)}, u32[]{:S(2)}) collective-permute-start(bf16[256,512]{1,0:T(8,128)(2,1)S(1)} %add_convert_fusion.2), channel_id=1, source_target_pairs={{0,192},{32,224},{64,0},{96,32},{128,64},{160,96},{192,128},{224,1... | collective-permute-start | bytes 786440 | tf_op jit(solution)/shard_map/ppermute | solution.py:14
  138.6 1.2 add_convert_fusion
  139.8 6.9 %collective-permute-done.3 = bf16[768,512]{1,0:T(8,128)(2,1)S(1)} collective-permute-done((bf16[768,512]{1,0:T(8,128)(2,1)}, bf16[768,512]{1,0:T(8,128)(2,1)S(1)}, u32[]{:S(2)}, u32[]{:S(2)}) %collective-permute-start.3) | collective-permute-done | bytes 786464 | tf_op jit(solution)/shard_map/ppermute | solution.py:14
  146.7 1.4 collective-permute-start.8
  148.2 9.7 %collective-permute-done.2 = bf16[256,512]{1,0:T(8,128)(2,1)S(1)} collective-permute-done((bf16[256,512]{1,0:T(8,128)(2,1)S(1)}, bf16[256,512]{1,0:T(8,128)(2,1)S(1)}, u32[]{:S(2)}, u32[]{:S(2)}) %collective-permute-start.2) | collective-permute-done | bytes 262176 | tf_op jit(solution)/shard_map/ppermute | solution.py:14
  158.0 0.5 collective-permute-done.8
  158.4 0.6 convert_add_fusion.1
  159.1 3.0 %collective-permute-start.9 = (bf16[128,1024]{1,0:T(8,128)(2,1)S(1)}, bf16[128,1024]{1,0:T(8,128)(2,1)S(1)}, u32[]{:S(2)}, u32[]{:S(2)}) collective-permute-start(bf16[128,1024]{1,0:T(8,128)(2,1)S(1)} %dynamic-slice_convert_fusion.1), channel_id=1, source_target_pairs={{0,32},{32,0},{64,96},{96,64},{128,160},{160,128},{192,224},{224,1... | collective-permute-start | bytes 786440 | tf_op jit(solution)/shard_map/ppermute | solution.py:18
  162.1 1.0 add_convert_fusion.1
  163.2 1.1 collective-permute-start.10
  164.2 1.7 collective-permute-start.11
  165.9 0.1 collective-permute-start.6
  166.1 2.1 %collective-permute-done.9 = bf16[128,1024]{1,0:T(8,128)(2,1)S(1)} collective-permute-done((bf16[128,1024]{1,0:T(8,128)(2,1)S(1)}, bf16[128,1024]{1,0:T(8,128)(2,1)S(1)}, u32[]{:S(2)}, u32[]{:S(2)}) %collective-permute-start.9) | collective-permute-done | bytes 262176 | tf_op jit(solution)/shard_map/ppermute | solution.py:18
  168.1 0.9 add_bitcast_fusion.1
  169.0 2.3 %collective-permute-done.10 = bf16[256,512]{1,0:T(8,128)(2,1)S(1)} collective-permute-done((bf16[256,512]{1,0:T(8,128)(2,1)S(1)}, bf16[256,512]{1,0:T(8,128)(2,1)S(1)}, u32[]{:S(2)}, u32[]{:S(2)}) %collective-permute-start.10) | collective-permute-done | bytes 262176 | tf_op jit(solution)/shard_map/ppermute | solution.py:14
  171.3 0.2 convert_add_fusion
  171.5 0.4 collective-permute-start.12
  171.9 0.9 collective-permute-done.6
  172.8 0.9 add_bitcast_fusion.2
  173.6 4.7 %collective-permute-done.12 = bf16[128,1024]{1,0:T(8,128)(2,1)S(1)} collective-permute-done((bf16[128,1024]{1,0:T(8,128)(2,1)S(1)}, bf16[128,1024]{1,0:T(8,128)(2,1)S(1)}, u32[]{:S(2)}, u32[]{:S(2)}) %collective-permute-start.12) | collective-permute-done | bytes 262176 | tf_op jit(solution)/shard_map/ppermute | solution.py:18
  178.3 0.9 add_bitcast_fusion
  179.2 1.5 shard_map.112
  180.6 0.5 convert_reduce_fusion
  (25 shorter events, 0.3 us)
Async XLA Ops:
  1.3 1.0 copy-start.8
  2.3 1.0 copy-start.9
  3.4 0.7 copy-start.10
  5.2 85.5 %copy-start.3 = (bf16[1,1024,1024]{2,1,0:T(8,128)(2,1)S(1)}, bf16[1,1024,1024]{2,1,0:T(8,128)(2,1)}, u32[]{:S(2)}) copy-start(bf16[1,1024,1024]{2,1,0:T(8,128)(2,1)} %param.11) | copy-start | bytes 6291460
  5.2 85.5 %copy-start.4 = (bf16[1,1024,1024]{2,1,0:T(8,128)(2,1)S(1)}, bf16[1,1024,1024]{2,1,0:T(8,128)(2,1)}, u32[]{:S(2)}) copy-start(bf16[1,1024,1024]{2,1,0:T(8,128)(2,1)} %param.12) | copy-start | bytes 6291460
  5.2 85.5 %copy-start.5 = (bf16[1,1024,1024]{2,1,0:T(8,128)(2,1)S(1)}, bf16[1,1024,1024]{2,1,0:T(8,128)(2,1)}, u32[]{:S(2)}) copy-start(bf16[1,1024,1024]{2,1,0:T(8,128)(2,1)} %param.13) | copy-start | bytes 6291460
  105.9 1.6 copy-start
  107.5 1.2 copy-start.2
  108.7 0.9 copy-start.6
  109.6 0.9 copy-start.7
  110.5 19.5 %collective-permute-start = (bf16[768,512]{1,0:T(8,128)(2,1)}, bf16[768,512]{1,0:T(8,128)(2,1)}, u32[]{:S(2)}, u32[]{:S(2)}) collective-permute-start(bf16[768,512]{1,0:T(8,128)(2,1)} %get-tuple-element.41), channel_id=1, source_target_pairs={{0,64},{32,96},{64,128},{96,160},{128,192},{160,224},{192,0},{224,... | collective-permute-start | bytes 2359304 | tf_op jit(solution)/shard_map/ppermute | solution.py:14
  112.1 18.4 %collective-permute-start.1 = (bf16[768,512]{1,0:T(8,128)(2,1)}, bf16[768,512]{1,0:T(8,128)(2,1)}, u32[]{:S(2)}, u32[]{:S(2)}) collective-permute-start(bf16[768,512]{1,0:T(8,128)(2,1)} %get-tuple-element.42), channel_id=1, source_target_pairs={{0,192},{32,224},{64,0},{96,32},{128,64},{160,96},{192,128},{224,1... | collective-permute-start | bytes 2359304 | tf_op jit(solution)/shard_map/ppermute | solution.py:14
  113.3 65.8 %all-to-all-start.1 = ((bf16[32,24,1152]{2,1,0:T(8,128)(2,1)}), bf16[32,24,1152]{2,1,0:T(8,128)(2,1)S(1)}, u32[]{:S(2)}, u32[]{:S(2)}) async-start(bf16[32,24,1152]{2,1,0:T(8,128)(2,1)} %bitcast.8), calls=%async_computation.1 | async-start | bytes 3538944 | tf_op jit(solution)/shard_map/all_to_all | solution.py:195
  120.0 26.7 %collective-permute-start.3 = (bf16[768,512]{1,0:T(8,128)(2,1)}, bf16[768,512]{1,0:T(8,128)(2,1)S(1)}, u32[]{:S(2)}, u32[]{:S(2)}) collective-permute-start(bf16[768,512]{1,0:T(8,128)(2,1)} %copy-done.7), channel_id=1, source_target_pairs={{0,64},{32,96},{64,128},{96,160},{128,192},{160,224},{192,0},{224,... | collective-permute-start | bytes 2359304 | tf_op jit(solution)/shard_map/ppermute | solution.py:14
  120.2 28.0 %collective-permute-start.4 = (bf16[768,512]{1,0:T(8,128)(2,1)}, bf16[768,512]{1,0:T(8,128)(2,1)S(1)}, u32[]{:S(2)}, u32[]{:S(2)}) collective-permute-start(bf16[768,512]{1,0:T(8,128)(2,1)} %copy-done.6), channel_id=1, source_target_pairs={{0,192},{32,224},{64,0},{96,32},{128,64},{160,96},{192,128},{224,1... | collective-permute-start | bytes 2359304 | tf_op jit(solution)/shard_map/ppermute | solution.py:14
  132.5 25.5 %collective-permute-start.7 = (bf16[256,512]{1,0:T(8,128)(2,1)S(1)}, bf16[256,512]{1,0:T(8,128)(2,1)S(1)}, u32[]{:S(2)}, u32[]{:S(2)}) collective-permute-start(bf16[256,512]{1,0:T(8,128)(2,1)S(1)} %add_convert_fusion.5), channel_id=1, source_target_pairs={{0,64},{32,96},{64,128},{96,160},{128,192},{160,224},{192,0},{224,... | collective-permute-start | bytes 786440 | tf_op jit(solution)/shard_map/ppermute | solution.py:14
  135.8 22.1 %collective-permute-start.2 = (bf16[256,512]{1,0:T(8,128)(2,1)S(1)}, bf16[256,512]{1,0:T(8,128)(2,1)S(1)}, u32[]{:S(2)}, u32[]{:S(2)}) collective-permute-start(bf16[256,512]{1,0:T(8,128)(2,1)S(1)} %add_convert_fusion.3), channel_id=1, source_target_pairs={{0,64},{32,96},{64,128},{96,160},{128,192},{160,224},{192,0},{224,... | collective-permute-start | bytes 786440 | tf_op jit(solution)/shard_map/ppermute | solution.py:14
  136.2 21.7 %collective-permute-start.5 = (bf16[256,512]{1,0:T(8,128)(2,1)S(1)}, bf16[256,512]{1,0:T(8,128)(2,1)S(1)}, u32[]{:S(2)}, u32[]{:S(2)}) collective-permute-start(bf16[256,512]{1,0:T(8,128)(2,1)S(1)} %add_convert_fusion.2), channel_id=1, source_target_pairs={{0,192},{32,224},{64,0},{96,32},{128,64},{160,96},{192,128},{224,1... | collective-permute-start | bytes 786440 | tf_op jit(solution)/shard_map/ppermute | solution.py:14
  138.6 19.8 %copy-start.1 = (f32[768,1024]{1,0:T(8,128)S(1)}, f32[768,1024]{1,0:T(8,128)}, u32[]{:S(2)}) copy-start(f32[768,1024]{1,0:T(8,128)} %copy-done) | copy-start | bytes 9437188
  146.7 11.7 %collective-permute-start.8 = (bf16[256,512]{1,0:T(8,128)(2,1)S(1)}, bf16[256,512]{1,0:T(8,128)(2,1)S(1)}, u32[]{:S(2)}, u32[]{:S(2)}) collective-permute-start(bf16[256,512]{1,0:T(8,128)(2,1)S(1)} %add_convert_fusion.4), channel_id=1, source_target_pairs={{0,192},{32,224},{64,0},{96,32},{128,64},{160,96},{192,128},{224,1... | collective-permute-start | bytes 786440 | tf_op jit(solution)/shard_map/ppermute | solution.py:14
  159.1 9.0 %collective-permute-start.9 = (bf16[128,1024]{1,0:T(8,128)(2,1)S(1)}, bf16[128,1024]{1,0:T(8,128)(2,1)S(1)}, u32[]{:S(2)}, u32[]{:S(2)}) collective-permute-start(bf16[128,1024]{1,0:T(8,128)(2,1)S(1)} %dynamic-slice_convert_fusion.1), channel_id=1, source_target_pairs={{0,32},{32,0},{64,96},{96,64},{128,160},{160,128},{192,224},{224,1... | collective-permute-start | bytes 786440 | tf_op jit(solution)/shard_map/ppermute | solution.py:18
  163.2 8.1 %collective-permute-start.10 = (bf16[256,512]{1,0:T(8,128)(2,1)S(1)}, bf16[256,512]{1,0:T(8,128)(2,1)S(1)}, u32[]{:S(2)}, u32[]{:S(2)}) collective-permute-start(bf16[256,512]{1,0:T(8,128)(2,1)S(1)} %add_convert_fusion.1), channel_id=1, source_target_pairs={{0,64},{32,96},{64,128},{96,160},{128,192},{160,224},{192,0},{224,... | collective-permute-start | bytes 786440 | tf_op jit(solution)/shard_map/ppermute | solution.py:14
  164.2 7.0 %collective-permute-start.11 = (bf16[256,512]{1,0:T(8,128)(2,1)S(1)}, bf16[256,512]{1,0:T(8,128)(2,1)S(1)}, u32[]{:S(2)}, u32[]{:S(2)}) collective-permute-start(bf16[256,512]{1,0:T(8,128)(2,1)S(1)} %add_convert_fusion), channel_id=1, source_target_pairs={{0,192},{32,224},{64,0},{96,32},{128,64},{160,96},{192,128},{224,1... | collective-permute-start | bytes 786440 | tf_op jit(solution)/shard_map/ppermute | solution.py:14
  165.9 6.8 %collective-permute-start.6 = (bf16[128,1024]{1,0:T(8,128)(2,1)S(1)}, bf16[128,1024]{1,0:T(8,128)(2,1)S(1)}, u32[]{:S(2)}, u32[]{:S(2)}) collective-permute-start(bf16[128,1024]{1,0:T(8,128)(2,1)S(1)} %dynamic-slice_convert_fusion.2), channel_id=1, source_target_pairs={{0,32},{32,0},{64,96},{96,64},{128,160},{160,128},{192,224},{224,1... | collective-permute-start | bytes 786440 | tf_op jit(solution)/shard_map/ppermute | solution.py:18
  171.5 6.8 %collective-permute-start.12 = (bf16[128,1024]{1,0:T(8,128)(2,1)S(1)}, bf16[128,1024]{1,0:T(8,128)(2,1)S(1)}, u32[]{:S(2)}, u32[]{:S(2)}) collective-permute-start(bf16[128,1024]{1,0:T(8,128)(2,1)S(1)} %dynamic-slice_convert_fusion), channel_id=1, source_target_pairs={{0,32},{32,0},{64,96},{96,64},{128,160},{160,128},{192,224},{224,1... | collective-permute-start | bytes 786440 | tf_op jit(solution)/shard_map/ppermute | solution.py:18

commit v4 on v3

--- a/solution.py
+++ b/solution.py
@@ -97,13 +97,14 @@
         grad = grad + product(up_pre[...], w_up[cut, :], RIGHT_TURNED)
         leaving[:, cut] = grad.astype(jnp.bfloat16)
     for cut, (left, right) in zip(cuts, pairs):
-        own[cut, :] = product(columns_of(left, y, 0), right[...], LEFT_TURNED)
+        part = product(columns_of(left, y, 0), right[...], LEFT_TURNED)
+        own[cut, :] = part.astype(jnp.bfloat16)
     for cut, (left, right) in zip(cuts, pairs):
         part = product(columns_of(left, y, 1), right[...], LEFT_TURNED)
-        add_up[cut, :] = part[:, :HALF]
+        add_up[cut, :] = part[:, :HALF].astype(jnp.bfloat16)
         ready_up[cut, :] = part[:, HALF:].astype(jnp.bfloat16)
         part = product(columns_of(left, y, 3), right[...], LEFT_TURNED)
-        add_down[cut, :] = part[:, HALF:]
+        add_down[cut, :] = part[:, HALF:].astype(jnp.bfloat16)
         ready_down[cut, :] = part[:, :HALF].astype(jnp.bfloat16)
 
 
@@ -111,9 +112,8 @@
     slots, width = both.shape[0], w_gate.shape[0]
     size = w_gate.shape[1]
     shapes = [((slots, width + NOTES), jnp.bfloat16)]
-    shapes += [((3 * BLOCK, HALF), jnp.bfloat16)] * 4
-    shapes += [((3 * BLOCK, HALF), jnp.float32)] * 2
-    shapes += [((3 * BLOCK, width), jnp.float32)]
+    shapes += [((3 * BLOCK, HALF), jnp.bfloat16)] * 6
+    shapes += [((3 * BLOCK, width), jnp.bfloat16)]
     in_vmem = pl.BlockSpec(memory_space=pltpu.VMEM)
     return pl.pallas_call(
         expert_kernel,
@@ -167,15 +167,15 @@
 
 
 def second_values(up_part, down_part, got):
-    up_part = (up_part + got[0].astype(jnp.float32)).astype(jnp.bfloat16)
-    down_part = (down_part + got[1].astype(jnp.float32)).astype(jnp.bfloat16)
+    up_part = (up_part.astype(jnp.float32) + got[0].astype(jnp.float32)).astype(jnp.bfloat16)
+    down_part = (down_part.astype(jnp.float32) + got[1].astype(jnp.float32)).astype(jnp.bfloat16)
     return lax.optimization_barrier((up_part, down_part))
 
 
 def third_step(own, ready, added, low):
     left = jnp.concatenate([added[0], ready[0]], axis=1)
     right = jnp.concatenate([ready[1], added[1]], axis=1)
-    total = own + left.astype(jnp.float32) + right.astype(jnp.float32)
+    total = own.astype(jnp.float32) + left.astype(jnp.float32) + right.astype(jnp.float32)
     away = lax.dynamic_slice_in_dim(total, (1 - low) * 128, 128, axis=0)
     keep = lax.dynamic_slice_in_dim(total, low * 128, 128, axis=0)
     return (keep + swap_low(away.astype(jnp.bfloat16)).astype(jnp.float32))[None]
@@ -230,10 +230,6 @@
             *after((add_up[cut], add_down[cut]), values), [value[cut] for value in got]
         )
         second.append((shift_y(values[0], 1), shift_y(values[1], -1)))
-    parts = []
-    for place, (cut, added) in enumerate(zip(cuts, second)):
-        mine = after(own[cut], parts[0]) if place == 2 else own[cut]
-        parts.append(third_step(mine, [value[cut] for value in ready], added, low))
     grad_tokens, grad_prob = call(
         home_kernel,
         (
@@ -244,6 +240,11 @@
         (slot, weight, home),
         2 * count * slots * width,
     )
+    parts = []
+    for place, (cut, added) in enumerate(zip(cuts, second)):
+        ahead = (*parts, grad_tokens) if place == 2 else values
+        mine = after(own[cut], ahead)
+        parts.append(third_step(mine, [value[cut] for value in ready], added, low))
     grad_prob = grad_prob.reshape(count).astype(jnp.bfloat16)
     return (grad_tokens, grad_prob, parts[1], parts[2], parts[0])
 

time: 182 us -> 186 us (1.022)
  other arithmetic: 10.9 us -> 15.1 us
  waiting for transfers between devices: 32.7 us -> 28.9 us
  local copies, waits for them, and re-layouts: 9.54 us -> 12.8 us
    ppermute x10, waiting for transfers between devices: 25.2 us -> 18.8 us  [shift_y(): return lax.ppermute(value, 'dp', pairs)]
    ppermute x3, waiting for transfers between devices: 7.56 us -> 10.1 us  [swap_low(): return lax.ppermute(value, 'dp', [(dp, dp ^ 1) for dp in range(8)])]
    broadcast_in_dim x3, other arithmetic: 2.59 us -> 4.64 us  [third_step(): (keep + swap_low(away.astype(jnp.bfloat16)).astype(jnp.float32))[None]]
    unnamed x22 -> x24, local copies, waits for them, and re-layouts: 7.4 us -> 7.35 us
  transfers between devices with their start and end apart: 14 -> 14, of which waited for: 9 -> 8; matrix products, arithmetic and copies ran while one was open for 7% -> 9% of each run, Pallas kernels for 0% -> 1%
where the time goes in v4:
time: 186 us; the launch traced here: 185 us
  blocking collectives  85.4 us (46%)
  waiting for transfers between devices  28.9 us (16%)
  starting transfers between devices  24.5 us (13%)
  Pallas kernels  17.8 us (10%)
  other arithmetic  15.1 us (8%)
  local copies, waits for them, and re-layouts  12.8 us (7%)
    all_to_all x1, blocking collectives, exchange(): lax.all_to_all(blocks, 'expert', split_axis=0, concat_axis=0, tiled=True)  85.4 us
    ppermute x10, waiting for transfers between devices, shift_y(): return lax.ppermute(value, 'dp', pairs)  18.8 us
    pallas_call x1, Pallas kernels, expert(): pl.pallas_call(expert_kernel, out_shape=[jax.ShapeDtypeStruct(*shape) for...  15.2 us
    ppermute x10, starting transfers between devices, shift_y(): return lax.ppermute(value, 'dp', pairs)  13.7 us
    ppermute x3, waiting for transfers between devices, swap_low(): return lax.ppermute(value, 'dp', [(dp, dp ^ 1) for dp in range(8)])  10.1 us
    unnamed x24, local copies, waits for them, and re-layouts  7.35 us
    all_to_all x1, starting transfers between devices, exchange(): lax.all_to_all(blocks, 'expert', split_axis=0, concat_axis=0, tiled=True)  6.68 us
    broadcast_in_dim x3, other arithmetic, third_step(): (keep + swap_low(away.astype(jnp.bfloat16)).astype(jnp.float32))[None]  4.64 us
  transfers between devices with their start and end apart: 14, of which 8 were waited for; matrix products, arithmetic and copies ran while one was open for 9% of the time, Pallas kernels for 1%

profile of v4, /device:TPU:1, one launch (start us, length us, event | category | flops | bytes accessed | tf_op | source)
XLA Modules:
  0.0 185.2 jit_solution(10628868552804700359)
XLA Ops:
  0.6 0.7 reshape.43
  1.3 1.0 copy-done.7
  2.3 1.0 copy-done.8
  3.4 0.7 copy-done.9
  4.1 1.1 shard_map.110
  5.2 85.4 %all_to_all.10 = bf16[32,24,2048]{2,1,0:T(8,128)(2,1)S(1)} all-to-all(bf16[32,24,2048]{2,1,0:T(8,128)(2,1)S(1)} %bitcast.18), channel_id=1, replica_groups=mesh['dp'=8,'expert'=32] {'expert'}, dimensions={0} | all-to-all | bytes 6291456 | tf_op jit(solution)/shard_map/all_to_all | solution.py:195
  90.6 15.2 %shard_map.111 = (bf16[768,1152]{1,0:T(8,128)(2,1)}, bf16[768,512]{1,0:T(8,128)(2,1)}, bf16[768,512]{1,0:T(8,128)(2,1)}, bf16[768,512]{1,0:T(8,128)(2,1)S(1)}, b...) custom-call(s32[1]{0:T(128)} %bitcast.position, ...), custom_call_target="tpu_custom_call" | custom-call | flops 12884901888 | bytes 20000000 | tf_op jit(solution)/shard_map/pallas_call | solution.py:118
  105.8 0.9 copy-done
  106.7 0.9 copy-done.1
  107.6 0.9 copy-done.5
  108.5 0.9 copy-done.6
  109.4 1.5 collective-permute-start
  111.0 1.3 collective-permute-start.1
  112.2 6.7 %all-to-all-start.1 = ((bf16[32,24,1152]{2,1,0:T(8,128)(2,1)}), bf16[32,24,1152]{2,1,0:T(8,128)(2,1)S(1)}, u32[]{:S(2)}, u32[]{:S(2)}) async-start(bf16[32,24,1152]{2,1,0:T(8,128)(2,1)} %bitcast.8), calls=%async_computation.1 | async-start | bytes 3538944 | tf_op jit(solution)/shard_map/all_to_all | solution.py:195
  119.1 2.6 %collective-permute-start.4 = (bf16[768,512]{1,0:T(8,128)(2,1)}, bf16[768,512]{1,0:T(8,128)(2,1)S(1)}, u32[]{:S(2)}, u32[]{:S(2)}) collective-permute-start(bf16[768,512]{1,0:T(8,128)(2,1)} %copy-done.5), channel_id=1, source_target_pairs={{0,192},{32,224},{64,0},{96,32},{128,64},{160,96},{192,128},{224,1... | collective-permute-start | bytes 2359304 | tf_op jit(solution)/shard_map/ppermute | solution.py:14
  121.7 1.4 fusion.3
  123.1 0.9 fusion
  124.1 4.8 %collective-permute-done = bf16[768,512]{1,0:T(8,128)(2,1)} collective-permute-done((bf16[768,512]{1,0:T(8,128)(2,1)}, bf16[768,512]{1,0:T(8,128)(2,1)}, u32[]{:S(2)}, u32[]{:S(2)}) %collective-permute-start) | collective-permute-done | bytes 786464 | tf_op jit(solution)/shard_map/ppermute | solution.py:14
  129.3 1.0 add_convert_fusion.5
  130.3 1.0 add_convert_fusion.4
  131.4 1.3 collective-permute-start.7
  132.6 1.0 add_convert_fusion.3
  133.7 1.0 add_convert_fusion.2
  135.1 2.4 %collective-permute-start.5 = (bf16[256,512]{1,0:T(8,128)(2,1)S(1)}, bf16[256,512]{1,0:T(8,128)(2,1)S(1)}, u32[]{:S(2)}, u32[]{:S(2)}) collective-permute-start(bf16[256,512]{1,0:T(8,128)(2,1)S(1)} %add_convert_fusion.2), channel_id=1, source_target_pairs={{0,192},{32,224},{64,0},{96,32},{128,64},{160,96},{192,128},{224,1... | collective-permute-start | bytes 786440 | tf_op jit(solution)/shard_map/ppermute | solution.py:14
  137.4 1.7 add_convert_fusion
  139.2 6.4 %collective-permute-done.3 = bf16[768,512]{1,0:T(8,128)(2,1)S(1)} collective-permute-done((bf16[768,512]{1,0:T(8,128)(2,1)}, bf16[768,512]{1,0:T(8,128)(2,1)S(1)}, u32[]{:S(2)}, u32[]{:S(2)}) %collective-permute-start.3) | collective-permute-done | bytes 786464 | tf_op jit(solution)/shard_map/ppermute | solution.py:14
  145.6 1.4 collective-permute-start.8
  147.0 0.8 fusion.2
  147.8 1.7 add_convert_fusion.1
  149.5 0.8 fusion.1
  150.2 1.0 collective-permute-done.7
  151.2 6.1 %collective-permute-done.8 = bf16[256,512]{1,0:T(8,128)(2,1)S(1)} collective-permute-done((bf16[256,512]{1,0:T(8,128)(2,1)S(1)}, bf16[256,512]{1,0:T(8,128)(2,1)S(1)}, u32[]{:S(2)}, u32[]{:S(2)}) %collective-permute-start.8) | collective-permute-done | bytes 262176 | tf_op jit(solution)/shard_map/ppermute | solution.py:14
  157.5 0.7 dynamic-slice_convert_fusion.1
  158.2 2.9 %collective-permute-start.9 = (bf16[128,1024]{1,0:T(8,128)(2,1)}, bf16[128,1024]{1,0:T(8,128)(2,1)}, u32[]{:S(2)}, u32[]{:S(2)}) collective-permute-start(bf16[128,1024]{1,0:T(8,128)(2,1)} %dynamic-slice_convert_fusion.1), channel_id=1, source_target_pairs={{0,32},{32,0},{64,96},{96,64},{128,160},{160,128},{192,224},{224,1... | collective-permute-start | bytes 786440 | tf_op jit(solution)/shard_map/ppermute | solution.py:18
  161.3 1.0 copy-done.10
  162.3 0.7 dynamic-slice_convert_fusion.2
  163.0 1.1 collective-permute-start.10
  164.1 1.6 collective-permute-start.11
  165.7 1.6 collective-permute-done.9
  167.3 1.8 add_bitcast_fusion.1
  169.1 3.8 %collective-permute-done.6 = bf16[128,1024]{1,0:T(8,128)(2,1)} collective-permute-done((bf16[128,1024]{1,0:T(8,128)(2,1)}, bf16[128,1024]{1,0:T(8,128)(2,1)}, u32[]{:S(2)}, u32[]{:S(2)}) %collective-permute-start.6) | collective-permute-done | bytes 262176 | tf_op jit(solution)/shard_map/ppermute | solution.py:18
  172.9 2.0 %add_bitcast_fusion.2 = f32[1,128,1024]{2,1,0:T(8,128)} fusion(bf16[128,1024]{1,0:T(8,128)(2,1)} %collective-permute-done.6, f32[256,1024]{1,0:T(8,128)} %copy-done.10, s32[]{:T(128)S(6)} %select_n.23), kind=kLoop, calls=%fused_computation.7 | loop fusion | flops 262144 | bytes 1310724 | tf_op jit(solution)/shard_map/broadcast_in_dim | solution.py:181
  174.9 1.5 shard_map.112
  176.4 1.4 convert_add_fusion
  177.9 1.3 collective-permute-start.12
  179.1 0.5 convert_reduce_fusion
  179.7 4.7 %collective-permute-done.12 = bf16[128,1024]{1,0:T(8,128)(2,1)S(1)} collective-permute-done((bf16[128,1024]{1,0:T(8,128)(2,1)S(1)}, bf16[128,1024]{1,0:T(8,128)(2,1)S(1)}, u32[]{:S(2)}, u32[]{:S(2)}) %collective-permute-start.12) | collective-permute-done | bytes 262176 | tf_op jit(solution)/shard_map/ppermute | solution.py:18
  184.4 0.9 add_bitcast_fusion
  (29 shorter events, 1.5 us)
Async XLA Ops:
  1.3 1.0 copy-start.7
  2.3 1.0 copy-start.8
  3.4 0.7 copy-start.9
  5.2 85.5 %copy-start.2 = (bf16[1,1024,1024]{2,1,0:T(8,128)(2,1)S(1)}, bf16[1,1024,1024]{2,1,0:T(8,128)(2,1)}, u32[]{:S(2)}) copy-start(bf16[1,1024,1024]{2,1,0:T(8,128)(2,1)} %param.11) | copy-start | bytes 6291460
  5.2 85.5 %copy-start.3 = (bf16[1,1024,1024]{2,1,0:T(8,128)(2,1)S(1)}, bf16[1,1024,1024]{2,1,0:T(8,128)(2,1)}, u32[]{:S(2)}) copy-start(bf16[1,1024,1024]{2,1,0:T(8,128)(2,1)} %param.12) | copy-start | bytes 6291460
  5.2 85.5 %copy-start.4 = (bf16[1,1024,1024]{2,1,0:T(8,128)(2,1)S(1)}, bf16[1,1024,1024]{2,1,0:T(8,128)(2,1)}, u32[]{:S(2)}) copy-start(bf16[1,1024,1024]{2,1,0:T(8,128)(2,1)} %param.13) | copy-start | bytes 6291460
  105.8 0.9 copy-start
  106.7 0.9 copy-start.1
  107.6 0.9 copy-start.5
  108.5 0.9 copy-start.6
  109.4 19.4 %collective-permute-start = (bf16[768,512]{1,0:T(8,128)(2,1)}, bf16[768,512]{1,0:T(8,128)(2,1)}, u32[]{:S(2)}, u32[]{:S(2)}) collective-permute-start(bf16[768,512]{1,0:T(8,128)(2,1)} %get-tuple-element.43), channel_id=1, source_target_pairs={{0,64},{32,96},{64,128},{96,160},{128,192},{160,224},{192,0},{224,... | collective-permute-start | bytes 2359304 | tf_op jit(solution)/shard_map/ppermute | solution.py:14
  111.0 18.4 %collective-permute-start.1 = (bf16[768,512]{1,0:T(8,128)(2,1)}, bf16[768,512]{1,0:T(8,128)(2,1)}, u32[]{:S(2)}, u32[]{:S(2)}) collective-permute-start(bf16[768,512]{1,0:T(8,128)(2,1)} %get-tuple-element.44), channel_id=1, source_target_pairs={{0,192},{32,224},{64,0},{96,32},{128,64},{160,96},{192,128},{224,1... | collective-permute-start | bytes 2359304 | tf_op jit(solution)/shard_map/ppermute | solution.py:14
  112.2 62.7 %all-to-all-start.1 = ((bf16[32,24,1152]{2,1,0:T(8,128)(2,1)}), bf16[32,24,1152]{2,1,0:T(8,128)(2,1)S(1)}, u32[]{:S(2)}, u32[]{:S(2)}) async-start(bf16[32,24,1152]{2,1,0:T(8,128)(2,1)} %bitcast.8), calls=%async_computation.1 | async-start | bytes 3538944 | tf_op jit(solution)/shard_map/all_to_all | solution.py:195
  118.9 26.7 %collective-permute-start.3 = (bf16[768,512]{1,0:T(8,128)(2,1)}, bf16[768,512]{1,0:T(8,128)(2,1)S(1)}, u32[]{:S(2)}, u32[]{:S(2)}) collective-permute-start(bf16[768,512]{1,0:T(8,128)(2,1)} %copy-done.6), channel_id=1, source_target_pairs={{0,64},{32,96},{64,128},{96,160},{128,192},{160,224},{192,0},{224,... | collective-permute-start | bytes 2359304 | tf_op jit(solution)/shard_map/ppermute | solution.py:14
  119.1 30.4 %collective-permute-start.4 = (bf16[768,512]{1,0:T(8,128)(2,1)}, bf16[768,512]{1,0:T(8,128)(2,1)S(1)}, u32[]{:S(2)}, u32[]{:S(2)}) collective-permute-start(bf16[768,512]{1,0:T(8,128)(2,1)} %copy-done.5), channel_id=1, source_target_pairs={{0,192},{32,224},{64,0},{96,32},{128,64},{160,96},{192,128},{224,1... | collective-permute-start | bytes 2359304 | tf_op jit(solution)/shard_map/ppermute | solution.py:14
  131.4 19.9 %collective-permute-start.7 = (bf16[256,512]{1,0:T(8,128)(2,1)S(1)}, bf16[256,512]{1,0:T(8,128)(2,1)S(1)}, u32[]{:S(2)}, u32[]{:S(2)}) collective-permute-start(bf16[256,512]{1,0:T(8,128)(2,1)S(1)} %add_convert_fusion.5), channel_id=1, source_target_pairs={{0,64},{32,96},{64,128},{96,160},{128,192},{160,224},{192,0},{224,... | collective-permute-start | bytes 786440 | tf_op jit(solution)/shard_map/ppermute | solution.py:14
  134.7 26.4 %collective-permute-start.2 = (bf16[256,512]{1,0:T(8,128)(2,1)S(1)}, bf16[256,512]{1,0:T(8,128)(2,1)S(1)}, u32[]{:S(2)}, u32[]{:S(2)}) collective-permute-start(bf16[256,512]{1,0:T(8,128)(2,1)S(1)} %add_convert_fusion.3), channel_id=1, source_target_pairs={{0,64},{32,96},{64,128},{96,160},{128,192},{160,224},{192,0},{224,... | collective-permute-start | bytes 786440 | tf_op jit(solution)/shard_map/ppermute | solution.py:14
  135.1 26.0 %collective-permute-start.5 = (bf16[256,512]{1,0:T(8,128)(2,1)S(1)}, bf16[256,512]{1,0:T(8,128)(2,1)S(1)}, u32[]{:S(2)}, u32[]{:S(2)}) collective-permute-start(bf16[256,512]{1,0:T(8,128)(2,1)S(1)} %add_convert_fusion.2), channel_id=1, source_target_pairs={{0,192},{32,224},{64,0},{96,32},{128,64},{160,96},{192,128},{224,1... | collective-permute-start | bytes 786440 | tf_op jit(solution)/shard_map/ppermute | solution.py:14
  145.6 11.7 %collective-permute-start.8 = (bf16[256,512]{1,0:T(8,128)(2,1)S(1)}, bf16[256,512]{1,0:T(8,128)(2,1)S(1)}, u32[]{:S(2)}, u32[]{:S(2)}) collective-permute-start(bf16[256,512]{1,0:T(8,128)(2,1)S(1)} %add_convert_fusion.4), channel_id=1, source_target_pairs={{0,192},{32,224},{64,0},{96,32},{128,64},{160,96},{192,128},{224,1... | collective-permute-start | bytes 786440 | tf_op jit(solution)/shard_map/ppermute | solution.py:14
  158.2 9.1 %collective-permute-start.9 = (bf16[128,1024]{1,0:T(8,128)(2,1)}, bf16[128,1024]{1,0:T(8,128)(2,1)}, u32[]{:S(2)}, u32[]{:S(2)}) collective-permute-start(bf16[128,1024]{1,0:T(8,128)(2,1)} %dynamic-slice_convert_fusion.1), channel_id=1, source_target_pairs={{0,32},{32,0},{64,96},{96,64},{128,160},{160,128},{192,224},{224,1... | collective-permute-start | bytes 786440 | tf_op jit(solution)/shard_map/ppermute | solution.py:18
  161.3 1.0 copy-start.10
  163.0 9.9 %collective-permute-start.6 = (bf16[128,1024]{1,0:T(8,128)(2,1)}, bf16[128,1024]{1,0:T(8,128)(2,1)}, u32[]{:S(2)}, u32[]{:S(2)}) collective-permute-start(bf16[128,1024]{1,0:T(8,128)(2,1)} %dynamic-slice_convert_fusion.2), channel_id=1, source_target_pairs={{0,32},{32,0},{64,96},{96,64},{128,160},{160,128},{192,224},{224,1... | collective-permute-start | bytes 786440 | tf_op jit(solution)/shard_map/ppermute | solution.py:18
  163.0 13.4 %copy-start.11 = (bf16[256,1024]{1,0:T(8,128)(2,1)S(1)}, bf16[256,1024]{1,0:T(8,128)(2,1)}, u32[]{:S(2)}) copy-start(bf16[256,1024]{1,0:T(8,128)(2,1)} %get-tuple-element.62) | copy-start | bytes 1572868
  163.0 13.3 %collective-permute-start.10 = (bf16[256,512]{1,0:T(8,128)(2,1)}, bf16[256,512]{1,0:T(8,128)(2,1)}, u32[]{:S(2)}, u32[]{:S(2)}) collective-permute-start(bf16[256,512]{1,0:T(8,128)(2,1)} %add_convert_fusion.1), channel_id=1, source_target_pairs={{0,64},{32,96},{64,128},{96,160},{128,192},{160,224},{192,0},{224,... | collective-permute-start | bytes 786440 | tf_op jit(solution)/shard_map/ppermute | solution.py:14
  164.1 12.3 %collective-permute-start.11 = (bf16[256,512]{1,0:T(8,128)(2,1)}, bf16[256,512]{1,0:T(8,128)(2,1)}, u32[]{:S(2)}, u32[]{:S(2)}) collective-permute-start(bf16[256,512]{1,0:T(8,128)(2,1)} %add_convert_fusion), channel_id=1, source_target_pairs={{0,192},{32,224},{64,0},{96,32},{128,64},{160,96},{192,128},{224,1... | collective-permute-start | bytes 786440 | tf_op jit(solution)/shard_map/ppermute | solution.py:14
  177.9 6.5 %collective-permute-start.12 = (bf16[128,1024]{1,0:T(8,128)(2,1)S(1)}, bf16[128,1024]{1,0:T(8,128)(2,1)S(1)}, u32[]{:S(2)}, u32[]{:S(2)}) collective-permute-start(bf16[128,1024]{1,0:T(8,128)(2,1)S(1)} %dynamic-slice_convert_fusion), channel_id=1, source_target_pairs={{0,32},{32,0},{64,96},{96,64},{128,160},{160,128},{192,224},{224,1... | collective-permute-start | bytes 786440 | tf_op jit(solution)/shard_map/ppermute | solution.py:18

commit v5 on v4

--- a/solution.py
+++ b/solution.py
@@ -230,6 +230,10 @@
             *after((add_up[cut], add_down[cut]), values), [value[cut] for value in got]
         )
         second.append((shift_y(values[0], 1), shift_y(values[1], -1)))
+    parts = []
+    for place, (cut, added) in enumerate(zip(cuts, second)):
+        mine = after(own[cut], parts[0]) if place == 2 else after(own[cut], values)
+        parts.append(third_step(mine, [value[cut] for value in ready], added, low))
     grad_tokens, grad_prob = call(
         home_kernel,
         (
@@ -240,11 +244,6 @@
         (slot, weight, home),
         2 * count * slots * width,
     )
-    parts = []
-    for place, (cut, added) in enumerate(zip(cuts, second)):
-        ahead = (*parts, grad_tokens) if place == 2 else values
-        mine = after(own[cut], ahead)
-        parts.append(third_step(mine, [value[cut] for value in ready], added, low))
     grad_prob = grad_prob.reshape(count).astype(jnp.bfloat16)
     return (grad_tokens, grad_prob, parts[1], parts[2], parts[0])
 

time: 186 us -> 181 us (0.973)
  local copies, waits for them, and re-layouts: 12.8 us -> 8.1 us
  other arithmetic: 15.1 us -> 10.5 us
  waiting for transfers between devices: 28.9 us -> 33.1 us
    ppermute x10, waiting for transfers between devices: 18.8 us -> 23.6 us  [shift_y(): return lax.ppermute(value, 'dp', pairs)]
    ppermute x3, starting transfers between devices: 4.13 us -> 6.7 us  [swap_low(): return lax.ppermute(value, 'dp', [(dp, dp ^ 1) for dp in range(8)])]
    ppermute x10, starting transfers between devices: 13.7 us -> 11.5 us  [shift_y(): return lax.ppermute(value, 'dp', pairs)]
    broadcast_in_dim x3, other arithmetic: 4.64 us -> 2.56 us  [third_step(): (keep + swap_low(away.astype(jnp.bfloat16)).astype(jnp.float32))[None]]
    unnamed x24 -> x20, local copies, waits for them, and re-layouts: 7.35 us -> 6.31 us
  transfers between devices with their start and end apart: 14 -> 14, of which waited for: 8 -> 8; matrix products, arithmetic and copies ran while one was open for 9% -> 6% of each run, Pallas kernels for 1% -> 0%
where the time goes in v5:
time: 181 us
  blocking collectives  85.4 us (47%)
  waiting for transfers between devices  33.1 us (18%)
  starting transfers between devices  24.9 us (14%)
  Pallas kernels  17.8 us (10%)
  other arithmetic  10.5 us (6%)
  local copies, waits for them, and re-layouts  8.1 us (4%)
    all_to_all x1, blocking collectives, exchange(): lax.all_to_all(blocks, 'expert', split_axis=0, concat_axis=0, tiled=True)  85.4 us
    ppermute x10, waiting for transfers between devices, shift_y(): return lax.ppermute(value, 'dp', pairs)  23.6 us
    pallas_call x1, Pallas kernels, expert(): pl.pallas_call(expert_kernel, out_shape=[jax.ShapeDtypeStruct(*shape) for...  15.2 us
    ppermute x10, starting transfers between devices, shift_y(): return lax.ppermute(value, 'dp', pairs)  11.5 us
    ppermute x3, waiting for transfers between devices, swap_low(): return lax.ppermute(value, 'dp', [(dp, dp ^ 1) for dp in range(8)])  9.51 us
    ppermute x3, starting transfers between devices, swap_low(): return lax.ppermute(value, 'dp', [(dp, dp ^ 1) for dp in range(8)])  6.7 us
    all_to_all x1, starting transfers between devices, exchange(): lax.all_to_all(blocks, 'expert', split_axis=0, concat_axis=0, tiled=True)  6.68 us
    unnamed x20, local copies, waits for them, and re-layouts  6.31 us
  transfers between devices with their start and end apart: 14, of which 8 were waited for; matrix products, arithmetic and copies ran while one was open for 6% of the time, Pallas kernels for 0%

profile of v5, /device:TPU:1, one launch (start us, length us, event | category | flops | bytes accessed | tf_op | source)
XLA Modules:
  0.0 180.6 jit_solution(6751565462636535525)
XLA Ops:
  0.6 0.7 reshape.43
  1.3 1.0 copy-done.7
  2.3 1.0 copy-done.8
  3.4 0.7 copy-done.9
  4.1 1.1 shard_map.110
  5.2 85.4 %all_to_all.10 = bf16[32,24,2048]{2,1,0:T(8,128)(2,1)S(1)} all-to-all(bf16[32,24,2048]{2,1,0:T(8,128)(2,1)S(1)} %bitcast.18), channel_id=1, replica_groups=mesh['dp'=8,'expert'=32] {'expert'}, dimensions={0} | all-to-all | bytes 6291456 | tf_op jit(solution)/shard_map/all_to_all | solution.py:195
  90.6 15.2 %shard_map.111 = (bf16[768,1152]{1,0:T(8,128)(2,1)}, bf16[768,512]{1,0:T(8,128)(2,1)}, bf16[768,512]{1,0:T(8,128)(2,1)}, bf16[768,512]{1,0:T(8,128)(2,1)S(1)}, b...) custom-call(s32[1]{0:T(128)} %bitcast.position, ...), custom_call_target="tpu_custom_call" | custom-call | flops 12884901888 | bytes 20000000 | tf_op jit(solution)/shard_map/pallas_call | solution.py:118
  105.9 0.9 copy-done
  106.7 0.9 copy-done.1
  107.6 0.9 copy-done.5
  108.5 0.9 copy-done.6
  109.4 1.5 collective-permute-start
  110.9 1.3 collective-permute-start.1
  112.2 6.7 %all-to-all-start.1 = ((bf16[32,24,1152]{2,1,0:T(8,128)(2,1)}), bf16[32,24,1152]{2,1,0:T(8,128)(2,1)S(1)}, u32[]{:S(2)}, u32[]{:S(2)}) async-start(bf16[32,24,1152]{2,1,0:T(8,128)(2,1)} %bitcast.8), calls=%async_computation.1 | async-start | bytes 3538944 | tf_op jit(solution)/shard_map/all_to_all | solution.py:195
  118.9 0.2 collective-permute-start.3
  119.0 2.6 %collective-permute-start.4 = (bf16[768,512]{1,0:T(8,128)(2,1)}, bf16[768,512]{1,0:T(8,128)(2,1)S(1)}, u32[]{:S(2)}, u32[]{:S(2)}) collective-permute-start(bf16[768,512]{1,0:T(8,128)(2,1)} %copy-done.5), channel_id=1, source_target_pairs={{0,192},{32,224},{64,0},{96,32},{128,64},{160,96},{192,128},{224,1... | collective-permute-start | bytes 2359304 | tf_op jit(solution)/shard_map/ppermute | solution.py:14
  121.6 1.4 fusion.3
  123.1 0.1 fusion
  123.2 5.6 %collective-permute-done = bf16[768,512]{1,0:T(8,128)(2,1)} collective-permute-done((bf16[768,512]{1,0:T(8,128)(2,1)}, bf16[768,512]{1,0:T(8,128)(2,1)}, u32[]{:S(2)}, u32[]{:S(2)}) %collective-permute-start) | collective-permute-done | bytes 786464 | tf_op jit(solution)/shard_map/ppermute | solution.py:14
  128.8 0.5 collective-permute-done.1
  129.3 1.0 add_convert_fusion.5
  130.3 1.0 add_convert_fusion.4
  131.4 1.3 collective-permute-start.7
  132.6 1.5 collective-permute-start.8
  134.1 1.0 add_convert_fusion.3
  135.2 1.0 add_convert_fusion.2
  136.2 1.0 add_convert_fusion
  137.2 1.0 add_convert_fusion.1
  138.3 7.2 %collective-permute-done.3 = bf16[768,512]{1,0:T(8,128)(2,1)S(1)} collective-permute-done((bf16[768,512]{1,0:T(8,128)(2,1)}, bf16[768,512]{1,0:T(8,128)(2,1)S(1)}, u32[]{:S(2)}, u32[]{:S(2)}) %collective-permute-start.3) | collective-permute-done | bytes 786464 | tf_op jit(solution)/shard_map/ppermute | solution.py:14
  145.6 1.4 collective-permute-start.11
  147.0 0.4 collective-permute-start.2
  147.4 3.8 %collective-permute-done.7 = bf16[256,512]{1,0:T(8,128)(2,1)S(1)} collective-permute-done((bf16[256,512]{1,0:T(8,128)(2,1)S(1)}, bf16[256,512]{1,0:T(8,128)(2,1)S(1)}, u32[]{:S(2)}, u32[]{:S(2)}) %collective-permute-start.7) | collective-permute-done | bytes 262176 | tf_op jit(solution)/shard_map/ppermute | solution.py:14
  151.2 1.4 collective-permute-start.5
  152.6 0.2 convert_add_fusion.1
  152.8 3.6 %collective-permute-start.9 = (bf16[128,1024]{1,0:T(8,128)(2,1)S(1)}, bf16[128,1024]{1,0:T(8,128)(2,1)S(1)}, u32[]{:S(2)}, u32[]{:S(2)}) collective-permute-start(bf16[128,1024]{1,0:T(8,128)(2,1)S(1)} %dynamic-slice_convert_fusion.1), channel_id=1, source_target_pairs={{0,32},{32,0},{64,96},{96,64},{128,160},{160,128},{192,224},{224,1... | collective-permute-start | bytes 786440 | tf_op jit(solution)/shard_map/ppermute | solution.py:18
  156.4 6.0 %collective-permute-done.2 = bf16[256,512]{1,0:T(8,128)(2,1)S(1)} collective-permute-done((bf16[256,512]{1,0:T(8,128)(2,1)S(1)}, bf16[256,512]{1,0:T(8,128)(2,1)S(1)}, u32[]{:S(2)}, u32[]{:S(2)}) %collective-permute-start.2) | collective-permute-done | bytes 262176 | tf_op jit(solution)/shard_map/ppermute | solution.py:14
  162.4 0.5 collective-permute-done.5
  162.9 0.2 convert_add_fusion.2
  163.1 3.0 %collective-permute-start.6 = (bf16[128,1024]{1,0:T(8,128)(2,1)S(1)}, bf16[128,1024]{1,0:T(8,128)(2,1)S(1)}, u32[]{:S(2)}, u32[]{:S(2)}) collective-permute-start(bf16[128,1024]{1,0:T(8,128)(2,1)S(1)} %dynamic-slice_convert_fusion.2), channel_id=1, source_target_pairs={{0,32},{32,0},{64,96},{96,64},{128,160},{160,128},{192,224},{224,1... | collective-permute-start | bytes 786440 | tf_op jit(solution)/shard_map/ppermute | solution.py:18
  166.1 0.9 add_bitcast_fusion.1
  167.0 0.2 convert_add_fusion
  167.2 0.1 collective-permute-start.12
  167.4 4.7 %collective-permute-done.6 = bf16[128,1024]{1,0:T(8,128)(2,1)S(1)} collective-permute-done((bf16[128,1024]{1,0:T(8,128)(2,1)S(1)}, bf16[128,1024]{1,0:T(8,128)(2,1)S(1)}, u32[]{:S(2)}, u32[]{:S(2)}) %collective-permute-start.6) | collective-permute-done | bytes 262176 | tf_op jit(solution)/shard_map/ppermute | solution.py:18
  172.1 0.9 add_bitcast_fusion.2
  173.0 4.8 %collective-permute-done.12 = bf16[128,1024]{1,0:T(8,128)(2,1)S(1)} collective-permute-done((bf16[128,1024]{1,0:T(8,128)(2,1)S(1)}, bf16[128,1024]{1,0:T(8,128)(2,1)S(1)}, u32[]{:S(2)}, u32[]{:S(2)}) %collective-permute-start.12) | collective-permute-done | bytes 262176 | tf_op jit(solution)/shard_map/ppermute | solution.py:18
  177.7 0.9 add_bitcast_fusion
  178.6 1.5 shard_map.112
  180.1 0.5 convert_reduce_fusion
  (25 shorter events, 0.4 us)
Async XLA Ops:
  1.3 1.0 copy-start.7
  2.3 1.0 copy-start.8
  3.4 0.7 copy-start.9
  5.2 85.5 %copy-start.2 = (bf16[1,1024,1024]{2,1,0:T(8,128)(2,1)S(1)}, bf16[1,1024,1024]{2,1,0:T(8,128)(2,1)}, u32[]{:S(2)}) copy-start(bf16[1,1024,1024]{2,1,0:T(8,128)(2,1)} %param.11) | copy-start | bytes 6291460
  5.2 85.5 %copy-start.3 = (bf16[1,1024,1024]{2,1,0:T(8,128)(2,1)S(1)}, bf16[1,1024,1024]{2,1,0:T(8,128)(2,1)}, u32[]{:S(2)}) copy-start(bf16[1,1024,1024]{2,1,0:T(8,128)(2,1)} %param.12) | copy-start | bytes 6291460
  5.2 85.5 %copy-start.4 = (bf16[1,1024,1024]{2,1,0:T(8,128)(2,1)S(1)}, bf16[1,1024,1024]{2,1,0:T(8,128)(2,1)}, u32[]{:S(2)}) copy-start(bf16[1,1024,1024]{2,1,0:T(8,128)(2,1)} %param.13) | copy-start | bytes 6291460
  105.9 0.9 copy-start
  106.7 0.9 copy-start.1
  107.6 0.9 copy-start.5
  108.5 0.9 copy-start.6
  109.4 19.4 %collective-permute-start = (bf16[768,512]{1,0:T(8,128)(2,1)}, bf16[768,512]{1,0:T(8,128)(2,1)}, u32[]{:S(2)}, u32[]{:S(2)}) collective-permute-start(bf16[768,512]{1,0:T(8,128)(2,1)} %get-tuple-element.43), channel_id=1, source_target_pairs={{0,64},{32,96},{64,128},{96,160},{128,192},{160,224},{192,0},{224,... | collective-permute-start | bytes 2359304 | tf_op jit(solution)/shard_map/ppermute | solution.py:14
  110.9 18.4 %collective-permute-start.1 = (bf16[768,512]{1,0:T(8,128)(2,1)}, bf16[768,512]{1,0:T(8,128)(2,1)}, u32[]{:S(2)}, u32[]{:S(2)}) collective-permute-start(bf16[768,512]{1,0:T(8,128)(2,1)} %get-tuple-element.44), channel_id=1, source_target_pairs={{0,192},{32,224},{64,0},{96,32},{128,64},{160,96},{192,128},{224,1... | collective-permute-start | bytes 2359304 | tf_op jit(solution)/shard_map/ppermute | solution.py:14
  112.2 66.4 %all-to-all-start.1 = ((bf16[32,24,1152]{2,1,0:T(8,128)(2,1)}), bf16[32,24,1152]{2,1,0:T(8,128)(2,1)S(1)}, u32[]{:S(2)}, u32[]{:S(2)}) async-start(bf16[32,24,1152]{2,1,0:T(8,128)(2,1)} %bitcast.8), calls=%async_computation.1 | async-start | bytes 3538944 | tf_op jit(solution)/shard_map/all_to_all | solution.py:195
  118.9 26.7 %collective-permute-start.3 = (bf16[768,512]{1,0:T(8,128)(2,1)}, bf16[768,512]{1,0:T(8,128)(2,1)S(1)}, u32[]{:S(2)}, u32[]{:S(2)}) collective-permute-start(bf16[768,512]{1,0:T(8,128)(2,1)} %copy-done.6), channel_id=1, source_target_pairs={{0,64},{32,96},{64,128},{96,160},{128,192},{160,224},{192,0},{224,... | collective-permute-start | bytes 2359304 | tf_op jit(solution)/shard_map/ppermute | solution.py:14
  119.0 28.0 %collective-permute-start.4 = (bf16[768,512]{1,0:T(8,128)(2,1)}, bf16[768,512]{1,0:T(8,128)(2,1)S(1)}, u32[]{:S(2)}, u32[]{:S(2)}) collective-permute-start(bf16[768,512]{1,0:T(8,128)(2,1)} %copy-done.5), channel_id=1, source_target_pairs={{0,192},{32,224},{64,0},{96,32},{128,64},{160,96},{192,128},{224,1... | collective-permute-start | bytes 2359304 | tf_op jit(solution)/shard_map/ppermute | solution.py:14
  131.4 19.8 %collective-permute-start.7 = (bf16[256,512]{1,0:T(8,128)(2,1)S(1)}, bf16[256,512]{1,0:T(8,128)(2,1)S(1)}, u32[]{:S(2)}, u32[]{:S(2)}) collective-permute-start(bf16[256,512]{1,0:T(8,128)(2,1)S(1)} %add_convert_fusion.5), channel_id=1, source_target_pairs={{0,64},{32,96},{64,128},{96,160},{128,192},{160,224},{192,0},{224,... | collective-permute-start | bytes 786440 | tf_op jit(solution)/shard_map/ppermute | solution.py:14
  132.6 19.9 %collective-permute-start.8 = (bf16[256,512]{1,0:T(8,128)(2,1)S(1)}, bf16[256,512]{1,0:T(8,128)(2,1)S(1)}, u32[]{:S(2)}, u32[]{:S(2)}) collective-permute-start(bf16[256,512]{1,0:T(8,128)(2,1)S(1)} %add_convert_fusion.4), channel_id=1, source_target_pairs={{0,192},{32,224},{64,0},{96,32},{128,64},{160,96},{192,128},{224,1... | collective-permute-start | bytes 786440 | tf_op jit(solution)/shard_map/ppermute | solution.py:14
  138.2 28.8 %collective-permute-start.10 = (bf16[256,512]{1,0:T(8,128)(2,1)S(1)}, bf16[256,512]{1,0:T(8,128)(2,1)S(1)}, u32[]{:S(2)}, u32[]{:S(2)}) collective-permute-start(bf16[256,512]{1,0:T(8,128)(2,1)S(1)} %add_convert_fusion.1), channel_id=1, source_target_pairs={{0,64},{32,96},{64,128},{96,160},{128,192},{160,224},{192,0},{224,... | collective-permute-start | bytes 786440 | tf_op jit(solution)/shard_map/ppermute | solution.py:14
  145.6 21.4 %collective-permute-start.11 = (bf16[256,512]{1,0:T(8,128)(2,1)S(1)}, bf16[256,512]{1,0:T(8,128)(2,1)S(1)}, u32[]{:S(2)}, u32[]{:S(2)}) collective-permute-start(bf16[256,512]{1,0:T(8,128)(2,1)S(1)} %add_convert_fusion), channel_id=1, source_target_pairs={{0,192},{32,224},{64,0},{96,32},{128,64},{160,96},{192,128},{224,1... | collective-permute-start | bytes 786440 | tf_op jit(solution)/shard_map/ppermute | solution.py:14
  147.0 15.4 %collective-permute-start.2 = (bf16[256,512]{1,0:T(8,128)(2,1)S(1)}, bf16[256,512]{1,0:T(8,128)(2,1)S(1)}, u32[]{:S(2)}, u32[]{:S(2)}) collective-permute-start(bf16[256,512]{1,0:T(8,128)(2,1)S(1)} %add_convert_fusion.3), channel_id=1, source_target_pairs={{0,64},{32,96},{64,128},{96,160},{128,192},{160,224},{192,0},{224,... | collective-permute-start | bytes 786440 | tf_op jit(solution)/shard_map/ppermute | solution.py:14
  151.2 11.7 %collective-permute-start.5 = (bf16[256,512]{1,0:T(8,128)(2,1)S(1)}, bf16[256,512]{1,0:T(8,128)(2,1)S(1)}, u32[]{:S(2)}, u32[]{:S(2)}) collective-permute-start(bf16[256,512]{1,0:T(8,128)(2,1)S(1)} %add_convert_fusion.2), channel_id=1, source_target_pairs={{0,192},{32,224},{64,0},{96,32},{128,64},{160,96},{192,128},{224,1... | collective-permute-start | bytes 786440 | tf_op jit(solution)/shard_map/ppermute | solution.py:14
  152.8 13.3 %collective-permute-start.9 = (bf16[128,1024]{1,0:T(8,128)(2,1)S(1)}, bf16[128,1024]{1,0:T(8,128)(2,1)S(1)}, u32[]{:S(2)}, u32[]{:S(2)}) collective-permute-start(bf16[128,1024]{1,0:T(8,128)(2,1)S(1)} %dynamic-slice_convert_fusion.1), channel_id=1, source_target_pairs={{0,32},{32,0},{64,96},{96,64},{128,160},{160,128},{192,224},{224,1... | collective-permute-start | bytes 786440 | tf_op jit(solution)/shard_map/ppermute | solution.py:18
  163.1 9.0 %collective-permute-start.6 = (bf16[128,1024]{1,0:T(8,128)(2,1)S(1)}, bf16[128,1024]{1,0:T(8,128)(2,1)S(1)}, u32[]{:S(2)}, u32[]{:S(2)}) collective-permute-start(bf16[128,1024]{1,0:T(8,128)(2,1)S(1)} %dynamic-slice_convert_fusion.2), channel_id=1, source_target_pairs={{0,32},{32,0},{64,96},{96,64},{128,160},{160,128},{192,224},{224,1... | collective-permute-start | bytes 786440 | tf_op jit(solution)/shard_map/ppermute | solution.py:18
  167.2 10.5 %collective-permute-start.12 = (bf16[128,1024]{1,0:T(8,128)(2,1)S(1)}, bf16[128,1024]{1,0:T(8,128)(2,1)S(1)}, u32[]{:S(2)}, u32[]{:S(2)}) collective-permute-start(bf16[128,1024]{1,0:T(8,128)(2,1)S(1)} %dynamic-slice_convert_fusion), channel_id=1, source_target_pairs={{0,32},{32,0},{64,96},{96,64},{128,160},{160,128},{192,224},{224,1... | collective-permute-start | bytes 786440 | tf_op jit(solution)/shard_map/ppermute | solution.py:18
